TPU v7x, 128 devices: a whole 4x4x4 slice. The times are simulated.
128 devices in a mesh: seq: 16 (over y, z), hx: 8 (over x, core).
Axes of the slice: x: 4, y: 4, z: 4, core: 2. Of those that a mesh axis runs over, the one named last changes fastest.
Arguments:
- queries: bfloat16 [2048, 4096], P('seq', 'hx'), may hold values from -6 to 6
- keys: bfloat16 [2048, 4096], P('seq', 'hx'), may hold values from -6 to 6
- values: bfloat16 [2048, 4096], P('seq', 'hx'), may hold values from -6 to 6
- log_decay: float32 [2048, 32], P('seq', 'hx'), may hold values from -1 to 0
- doc_ids: int32 [2048], P('seq'), may hold values from 0 to 3, as said below
- residual: bfloat16 [2048, 6144], P('seq'), may hold values from -6 to 6
- out_weight: bfloat16 [4096, 6144], P('hx'), may hold values from -0.09375 to 0.09375
- norm_gain: float32 [6144], replicated, may hold values from 0.1 to 1.9
- expert_ids: int32 [2048, 2], P('seq'), may hold values from 0 to 7, all different within a row; in each aligned block of 128 rows (0 to 127, 128 to 255, ...) at most 40 rows name the same one
- route_weight: float32 [2048, 2], P('seq'), may hold values from 0.2 to 1
- w_gate: bfloat16 [8, 6144, 4608], P('hx', None, 'seq'), may hold values from -0.078125 to 0.078125
- w_up: bfloat16 [8, 6144, 4608], P('hx', None, 'seq'), may hold values from -0.078125 to 0.078125
- w_down: bfloat16 [8, 4608, 6144], P('hx', 'seq'), may hold values from -0.09375 to 0.09375
Outputs:
- layer_out: bfloat16 [2048, 6144], P('seq', 'hx')
Inputs may be any that keep to these rules, and one draw needn't show every extreme that they name: `expert_ids`: the two experts of a token differ; among the tokens of one sequence shard no expert is named more than 40 times, and some expert reaches 40. `doc_ids`: document numbers start at 0, never fall along the sequence, and rise by one at each of three positions.
All inputs are finite; a program needn't handle non-finite values.
Results may differ from a plain program's by a relative error of at most 0.022.
Values may be sent and summed in bfloat16 or wider, within the bound.
A program may use at most 128 MiB of HBM per device.

v0:
```python
import jax
import jax.numpy as jnp
from jax import lax
from jax.sharding import PartitionSpec as P

HS = 128


def prefix(shard, axis, join, neutral):
    place = lax.axis_index(axis)
    gathered = jax.tree.map(
        lambda a, kind: lax.all_gather(a.astype(kind), axis),
        shard,
        (jnp.bfloat16, jnp.bfloat16, jnp.bfloat16, jnp.bfloat16),
    )
    state = jax.tree.map(lambda a, e: jnp.zeros_like(a) + jnp.asarray(e, a.dtype), shard, neutral)

    def one(turn, state):
        return join(
            state,
            jax.tree.map(
                lambda a, own: lax.dynamic_index_in_dim(a, turn, 0, False).astype(own.dtype),
                gathered,
                shard,
            ),
        )

    return lax.fori_loop(0, place, one, state)


def link_states(earlier, later):
    through_one, state_one, first_one, last_one = earlier
    through_two, state_two, first_two, last_two = later
    passes = ((last_one < 0) | (first_two < 0) | (last_one == first_two)).astype(jnp.float32)
    through = through_one * through_two * passes
    head_state = passes * through_two[:, None, None] * state_one + state_two
    first_doc = jnp.where(first_one >= 0, first_one, first_two)
    last_doc = jnp.where(last_two >= 0, last_two, last_one)
    return (through, head_state, first_doc, last_doc)


def expert_act(row_block, w_gate, w_up):
    gate_part = jnp.dot(row_block, w_gate[0], preferred_element_type=jnp.float32)
    up_part = jnp.dot(row_block, w_up[0], preferred_element_type=jnp.float32)
    return (jax.nn.silu(gate_part) * up_part).astype(jnp.bfloat16)


def shards(
    queries,
    keys,
    values,
    log_decay,
    doc_ids,
    residual,
    out_weight,
    norm_gain,
    expert_ids,
    route_weight,
    w_gate,
    w_up,
    w_down,
):
    tok_count = queries.shape[0]
    heads_local = log_decay.shape[1]
    query_heads = queries.reshape(tok_count, heads_local, HS)
    key_heads = keys.reshape(tok_count, heads_local, HS)
    value_float = values.reshape(tok_count, heads_local, HS).astype(jnp.float32)
    log_cum = jnp.cumsum(log_decay, axis=0)
    positions = jnp.arange(tok_count)
    allowed = (positions[:, None] >= positions[None, :]) & (doc_ids[:, None] == doc_ids[None, :])
    exponent = jnp.where(allowed[None], log_cum.T[:, :, None] - log_cum.T[:, None, :], -jnp.inf)
    scores = jnp.einsum("thd,shd->hts", query_heads, key_heads, preferred_element_type=jnp.float32)
    intra = jnp.einsum(
        "hts,shd->thd", scores * jnp.exp(exponent), value_float, precision=lax.Precision.HIGHEST
    )
    first_doc = doc_ids[0]
    last_doc = doc_ids[tok_count - 1]
    end_weight = (
        jnp.exp(log_cum[tok_count - 1][None, :] - log_cum)
        * (doc_ids == last_doc).astype(jnp.float32)[:, None]
    )
    key_weighted = key_heads.astype(jnp.float32) * end_weight[:, :, None]
    head_state = jnp.einsum(
        "shi,shj->hij", key_weighted, value_float, precision=lax.Precision.HIGHEST
    )
    through = jnp.exp(log_cum[tok_count - 1]) * (first_doc == last_doc).astype(jnp.float32)
    first_float = jnp.full((1,), first_doc).astype(jnp.float32)
    last_float = jnp.full((1,), last_doc).astype(jnp.float32)
    identity = (
        jnp.ones((heads_local,), jnp.float32),
        jnp.zeros_like(head_state),
        jnp.full((1,), -1.0, jnp.float32),
        jnp.full((1,), -1.0, jnp.float32),
    )
    carried = prefix((through, head_state, first_float, last_float), "seq", link_states, identity)
    incoming = carried[1]
    before_doc = carried[3]
    entry_gate = (before_doc[0] == first_float[0]).astype(jnp.float32)
    carry_weight = (
        jnp.exp(log_cum) * (doc_ids == first_doc).astype(jnp.float32)[:, None] * entry_gate
    )
    query_weighted = query_heads.astype(jnp.float32) * carry_weight[:, :, None]
    carried_out = jnp.einsum(
        "thi,hij->thj", query_weighted, incoming, precision=lax.Precision.HIGHEST
    )
    head_out = intra + carried_out
    normed_heads = head_out * lax.rsqrt(
        jnp.mean(head_out * head_out, axis=-1, keepdims=True) + 1e-05
    )
    attn_in = normed_heads.reshape(tok_count, heads_local * HS).astype(jnp.bfloat16)
    expert_count = lax.axis_size("hx")
    capacity = tok_count * 5 // (2 * expert_count)
    flat_ids = expert_ids.reshape(-1)
    choice_count = flat_ids.shape[0]
    one_hot = (flat_ids[:, None] == jnp.arange(expert_count)[None, :]).astype(jnp.int32)
    rank_before = jnp.cumsum(one_hot, axis=0) - one_hot
    slot_index = flat_ids * capacity + jnp.sum(rank_before * one_hot, axis=1)
    token_of = jnp.arange(choice_count) // 2
    slot_match = slot_index[None, :] == jnp.arange(expert_count * capacity)[:, None]
    slot_valid = jnp.any(slot_match, axis=1)
    slot_token = jnp.sum(jnp.where(slot_match, token_of[None, :], 0), axis=1)
    expert_index = lax.axis_index("hx")
    first_slot = slot_index[0::2]
    second_slot = slot_index[1::2]
    row_block = jnp.where(slot_valid[:, None], attn_in[slot_token], jnp.zeros((), jnp.bfloat16))
    attn_slots = lax.psum_scatter(
        jnp.dot(row_block, out_weight, preferred_element_type=jnp.float32).astype(jnp.bfloat16),
        "hx",
        scatter_dimension=0,
        tiled=True,
    ).astype(jnp.float32)
    my_tokens = lax.dynamic_slice_in_dim(slot_token, expert_index * capacity, capacity)
    hidden_slots = residual[my_tokens].astype(jnp.float32) + attn_slots
    normed = (
        hidden_slots
        * lax.rsqrt(jnp.mean(hidden_slots * hidden_slots, axis=-1, keepdims=True) + 1e-06)
        * norm_gain
    ).astype(jnp.bfloat16)
    gathered = lax.all_gather(normed, "seq", axis=0, tiled=True)
    row_block = gathered
    act = expert_act(row_block, w_gate, w_up)
    expert_out = lax.psum_scatter(
        jnp.dot(act, w_down[0], preferred_element_type=jnp.float32).astype(jnp.bfloat16),
        "seq",
        scatter_dimension=0,
        tiled=True,
    ).astype(jnp.float32)
    back_hidden, back_expert = (
        lax.all_to_all(
            hidden_slots.astype(jnp.bfloat16), "hx", split_axis=1, concat_axis=0, tiled=True
        ).astype(hidden_slots.dtype),
        lax.all_to_all(
            expert_out.astype(jnp.bfloat16), "hx", split_axis=1, concat_axis=0, tiled=True
        ).astype(expert_out.dtype),
    )
    layer_out = (
        back_hidden[first_slot]
        + route_weight[:, 0:1] * back_expert[first_slot]
        + route_weight[:, 1:2] * back_expert[second_slot]
    )
    return layer_out.astype(jnp.bfloat16)


def solution(mesh):
    return jax.shard_map(
        shards,
        mesh=mesh,
        in_specs=(
            P("seq", "hx"),
            P("seq", "hx"),
            P("seq", "hx"),
            P("seq", "hx"),
            P("seq"),
            P("seq", None),
            P("hx", None),
            P(),
            P("seq", None),
            P("seq", None),
            P("hx", None, "seq"),
            P("hx", None, "seq"),
            P("hx", "seq", None),
        ),
        out_specs=P("seq", "hx"),
        check_vma=False,
    )
```

profile of v0, /device:TPU:1, one launch (start us, length us, event | category | flops | bytes accessed | tf_op | source)
XLA Modules:
  0.0 447.1 jit_solution(12811289903400545654)
XLA Ops:
  6.5 1.4 fusion.40
  9.3 2.5 compare_convert_fusion
  11.8 1.4 copy.69
  13.2 1.6 reduce_window_sum.28
  14.8 0.7 slice_bitcast_fusion.2
  15.5 1.6 exponential_multiply_fusion
  17.0 0.9 copy.75
  17.9 1.7 copy.85
  19.6 1.9 convolution_convert_fusion.2
  21.6 1.3 dynamic-slice
  22.8 1.4 dynamic-update-slice
  24.3 1.4 dynamic-update-slice.1
  25.7 36.4 %all-reduce.3 = (bf16[16]{0:T(256)(128)(2,1)}, bf16[16]{0:T(256)(128)(2,1)}) all-reduce(bf16[16]{0:T(256)(128)(2,1)S(1)} %dynamic-update-slice, bf16[16]{0:T(256)(128)(2,1)S(1)} %dynamic-update-slice.1), channel_id=2, replica_groups=mesh['seq'=16,'hx'=8] {'seq'}, use_global_device_ids=true, to_apply=%add | all-reduce | flops 32 | bytes 128
  62.0 13.7 %all-gather.3 = bf16[16,1,4]{2,1,0:T(2,128)(2,1)S(1)} all-gather(bf16[1,1,4]{2,1,0:T(2,128)(2,1)S(1)} %get-tuple-element.132), channel_id=1, replica_groups=mesh['seq'=16,'hx'=8] {'seq'}, dimensions={0}, use_global_device_ids=true | all-gather | bytes 136 | tf_op jit(solution)/shard_map/all_gather | solution.py:12
  76.4 1.4 copy.65
  77.8 1.5 reshape.211
  79.3 1.0 eq.79
  80.3 0.6 fusion.37
  80.9 1.2 reduce-window.6
  82.1 0.8 slice_reduce_fusion
  83.0 1.3 reduce-window.9
  84.2 1.3 slice.29
  85.5 1.5 copy.70
  87.0 0.6 copy.73
  87.6 0.7 copy.77
  88.3 0.8 fusion.36
  89.1 0.6 and_select_fusion
  89.9 0.7 fusion.17
  90.7 0.8 fusion.34
  91.5 1.1 convolution_multiply_fusion
  92.6 2.1 convolution_bitcast_fusion.1
  94.7 0.7 broadcast_in_dim.79
  95.4 1.6 multiply_multiply_fusion
  97.0 0.9 copy.79
  97.9 1.8 multiply_reduce_fusion.1
  99.7 0.7 multiply_convert_fusion.1
  100.4 1.6 copy.81
  102.0 3.5 gather_fusion.1
  105.6 7.0 %convolution_convert_fusion.1 = bf16[320,6144]{1,0:T(8,128)(2,1)} fusion(bf16[512,6144]{1,0:T(8,128)(2,1)} %param.21, bf16[320,512]{1,0:T(8,128)(2,1)} %gather_fusion.1, pred[320]{0:T(512)(128)(4,1)S(1)} %copy-done.6), kind=kOutput, calls=%fused_computation.13 | convolution fusion | flops 2015395840 | bytes 10551616 | tf_op jit(solution)/shard_map/dot_general | solution.py:127
  112.8 3.8 gather_fusion
  116.5 122.5 %reduce-scatter.5.cloned.1.call-done = bf16[40,6144]{1,0:T(8,128)(2,1)} async-done(((bf16[320,6144]{1,0:T(8,128)(2,1)}), bf16[40,6144]{1,0:T(8,128)(2,1)}) %reduce-scatter.5.cloned.1.call-update) | async-done | bytes 491536 | tf_op jit(solution)/shard_map/reduce_scatter | solution.py:126
  239.0 2.2 fusion.15
  241.3 2.2 multiply_convert_fusion
  243.5 0.2 reduce-scatter.7.cloned.1.call-start
  243.7 70.5 %all-gather.7.cloned.1.call-done = bf16[640,6144]{1,0:T(8,128)(2,1)} async-done(((bf16[40,6144]{1,0:T(8,128)(2,1)}), bf16[640,6144]{1,0:T(8,128)(2,1)}) %all-gather.7.cloned.1.call-update) | async-done | bytes 7864336 | tf_op jit(solution)/shard_map/all_gather | solution.py:139
  314.2 7.3 %fusion.6 = f32[640,288]{0,1:T(8,128)S(1)} fusion(bf16[640,6144]{1,0:T(8,128)(2,1)} %all-gather.7.cloned.1.call-done, bf16[1,6144,288]{1,2,0:T(8,128)(2,1)} %param.25), kind=kOutput, calls=%fused_computation.17 | convolution fusion | flops 2264924160 | bytes 12140544 | tf_op jit(solution)/shard_map/dot_general | solution.py:43
  321.7 2.9 fusion.11
  324.7 6.4 %convolution_convert_fusion = bf16[640,6144]{1,0:T(8,128)(2,1)} fusion(bf16[640,288]{0,1:T(8,128)(2,1)S(1)} %fusion.11, bf16[1,288,6144]{2,1,0:T(8,128)(2,1)S(1)} %copy-done), kind=kOutput, calls=%fused_computation.12 | convolution fusion | flops 2268856320 | bytes 11771904 | tf_op jit(solution)/shard_map/dot_general | solution.py:143
  331.1 0.6 copy-done.2
  331.8 0.2 slice.36
  332.0 0.2 slice.33
  332.2 1.9 copy.111
  334.1 4.9 %all-to-all-start = ((bf16[40,8,768]{2,0,1:T(8,128)(2,1)}), bf16[40,8,768]{2,0,1:T(8,128)(2,1)}, u32[]{:S(2)}, u32[]{:S(2)}) async-start(bf16[40,8,768]{2,0,1:T(8,128)(2,1)} %bitcast.120), calls=%async_computation.1 | async-start | bytes 983040 | tf_op jit(solution)/shard_map/all_to_all | solution.py:149
  339.1 74.3 %reduce-scatter.7.cloned.1.call-done = bf16[40,6144]{1,0:T(8,128)(2,1)} async-done(((bf16[640,6144]{1,0:T(8,128)(2,1)}), bf16[40,6144]{1,0:T(8,128)(2,1)}) %reduce-scatter.7.cloned.1.call-update) | async-done | bytes 491536
  413.3 1.9 copy.110
  415.2 6.2 %all-to-all-start.1 = ((bf16[40,8,768]{2,0,1:T(8,128)(2,1)}), bf16[40,8,768]{2,0,1:T(8,128)(2,1)}, u32[]{:S(2)}, u32[]{:S(2)}) async-start(bf16[40,8,768]{2,0,1:T(8,128)(2,1)} %bitcast.119), calls=%async_computation.2 | async-start | bytes 983040 | tf_op jit(solution)/shard_map/all_to_all | solution.py:152
  421.4 0.8 slice_bitcast_fusion.1
  422.2 2.0 convert_element_type.167
  424.2 2.9 gather_fusion.2
  427.1 3.5 all-to-all-done.1
  430.6 2.0 convert_element_type.168
  432.7 2.9 gather_fusion.3
  435.6 2.9 gather_fusion.4
  438.5 2.0 add_convert_fusion
  (36 shorter events, 0.6 us)
Async XLA Ops:
  6.5 318.1 %copy-start = (bf16[1,288,6144]{2,1,0:T(8,128)(2,1)S(1)}, bf16[1,288,6144]{2,1,0:T(8,128)(2,1)}, u32[]{:S(2)}) copy-start(bf16[1,288,6144]{2,1,0:T(8,128)(2,1)} %param.27) | copy-start | bytes 10616836
  6.5 88.2 %all-gather.9.cloned.1.call-start = ((), (), s32[]{:S(2)}) async-start(), calls=%async_computation.6 | async-start | bytes 2228224 | tf_op jit(solution)/shard_map/all_gather | solution.py:12
  21.5 217.5 %reduce-scatter.5.cloned.1.call-start = ((), (), s32[]{:S(2)}) async-start(), calls=%async_computation.4 | async-start | bytes 4423680 | tf_op jit(solution)/shard_map/reduce_scatter | solution.py:126
  89.7 0.9 copy-start.1
  89.9 5.5 %copy-start.3 = (f32[128]{0:T(128)S(1)}, f32[128]{0:T(128)}, u32[]{:S(2)}) copy-start(f32[128]{0:T(128)} %get-tuple-element.135) | copy-start | bytes 1540
  95.4 10.1 %copy-start.6 = (pred[320]{0:T(512)(128)(4,1)S(1)}, pred[320]{0:T(512)(128)(4,1)}, u32[]{:S(2)}) copy-start(pred[320]{0:T(512)(128)(4,1)} %fusion.17) | copy-start | bytes 964
  112.6 201.6 %all-gather.7.cloned.1.call-start = ((), (), s32[]{:S(2)}) async-start(), calls=%async_computation.5 | async-start | bytes 8355840 | tf_op jit(solution)/shard_map/all_gather | solution.py:139
  243.5 169.8 %reduce-scatter.7.cloned.1.call-start = ((), (), s32[]{:S(2)}) async-start(), calls=%async_computation.7 | async-start | bytes 8355840
  314.2 7.3 %copy-start.4 = (bf16[640,6144]{1,0:T(8,128)(2,1)S(1)}, bf16[640,6144]{1,0:T(8,128)(2,1)}, u32[]{:S(2)}) copy-start(bf16[640,6144]{1,0:T(8,128)(2,1)} %all-gather.7.cloned.1.call-done) | copy-start | bytes 23592964
  314.2 7.5 %copy-start.5 = (bf16[1,6144,288]{1,2,0:T(8,128)(2,1)S(1)}, bf16[1,6144,288]{1,2,0:T(8,128)(2,1)}, u32[]{:S(2)}) copy-start(bf16[1,6144,288]{1,2,0:T(8,128)(2,1)} %param.26) | copy-start | bytes 10616836
  331.1 0.7 copy-start.2
  334.1 81.1 %all-to-all-start = ((bf16[40,8,768]{2,0,1:T(8,128)(2,1)}), bf16[40,8,768]{2,0,1:T(8,128)(2,1)}, u32[]{:S(2)}, u32[]{:S(2)}) async-start(bf16[40,8,768]{2,0,1:T(8,128)(2,1)} %bitcast.120), calls=%async_computation.1 | async-start | bytes 983040 | tf_op jit(solution)/shard_map/all_to_all | solution.py:149
  415.2 15.4 %all-to-all-start.1 = ((bf16[40,8,768]{2,0,1:T(8,128)(2,1)}), bf16[40,8,768]{2,0,1:T(8,128)(2,1)}, u32[]{:S(2)}, u32[]{:S(2)}) async-start(bf16[40,8,768]{2,0,1:T(8,128)(2,1)} %bitcast.119), calls=%async_computation.2 | async-start | bytes 983040 | tf_op jit(solution)/shard_map/all_to_all | solution.py:152
Sparse Core Ops, SparseCore 0:
  21.6 47.4 all-gather.8
  112.7 126.2 reduce-scatter.4
  243.6 70.5 all-gather.6
  331.2 82.0 reduce-scatter.6
where the time goes:
time: 450 us; the launch traced here: 447 us
  waiting for transfers between devices  271 us (60%)
  blocking collectives  50.1 us (11%)
  local copies, waits for them, and re-layouts  42 us (9%)
  matrix products  30.6 us (7%)
  other arithmetic  27 us (6%)
  between operations  15.2 us (3%)
  starting transfers between devices  11.4 us (3%)
    reduce_scatter x1, waiting for transfers between devices, shards(): lax.psum_scatter(jnp.dot(row_block, out_weight, preferred_element_type=jn...  123 us
    unnamed x5, waiting for transfers between devices  74.3 us
    all_gather x1, waiting for transfers between devices, shards(): gathered = lax.all_gather(normed, 'seq', axis=0, tiled=True)  70.5 us
    unnamed x1, blocking collectives  36.4 us
    all_gather x1, blocking collectives, prefix(): lax.all_gather(a.astype(kind), axis)  13.7 us
  transfers between devices with their start and end apart: 6, of which 4 were waited for; matrix products, arithmetic and copies ran while one was open for 8% of the time, Pallas kernels for 0%

commit v1 on v0

--- a/solution.py
+++ b/solution.py
@@ -1,7 +1,294 @@
+import functools
 import jax
 import jax.numpy as jnp
 from jax import lax
+from jax.experimental import pallas as pl
+from jax.experimental.pallas import tpu as pltpu
 from jax.sharding import PartitionSpec as P
+
+MESH = pl.DeviceIdType.MESH
+CAP = 40
+SL = 8
+W = 768
+F = 288
+ORDER = [(0, 0), (1, 0), (3, 0), (0, 1), (0, 3), (1, 1), (1, 3), (3, 1), (3, 3), (2, 0), (0, 2), (1, 2), (3, 2), (2, 1), (2, 3), (2, 2)]
+SLOT = {r: i for i, r in enumerate(ORDER)}
+
+
+def at(half, first, second):
+    return SLOT[(first % 4, second % 4) if half == 0 else (second % 4, first % 4)]
+
+
+class Mail:
+    def __init__(self, send_sem, recv_sem):
+        self.send_sem, self.recv_sem = send_sem, recv_sem
+        self.number, self.sent = {}, []
+
+    def make(self, key, src, dst, device):
+        n = self.number.setdefault(key, len(self.number))
+        return pltpu.make_async_remote_copy(
+            src_ref=src, dst_ref=dst, send_sem=self.send_sem.at[n], recv_sem=self.recv_sem.at[n],
+            device_id=device, device_id_type=MESH)
+
+    def send(self, key, src, dst, device):
+        copy = self.make(key, src, dst, device)
+        copy.start()
+        self.sent.append(copy)
+
+    def arrived(self, key, dst, device):
+        self.make(key, dst, dst, device).wait_recv()
+
+    def drain(self):
+        for copy in self.sent:
+            copy.wait_send()
+
+
+def ring(half, seq):
+    y, z = seq // 4, seq % 4
+    yp, ym = ((y + 1) % 4) * 4 + z, ((y + 3) % 4) * 4 + z
+    zp, zm = y * 4 + (z + 1) % 4, y * 4 + (z + 3) % 4
+    ids = (yp, ym, zp, zm) if half == 0 else (zp, zm, yp, ym)
+    return [{"seq": i} for i in ids]
+
+
+class Gather:
+    def __init__(self, mail, x, half, seq):
+        self.mail, self.x, self.half = mail, x, half
+        self.fp, self.fm, self.sp, self.sm = ring(half, seq)
+
+    def part(self, f, s, unit):
+        lo, n = (4 * self.half, 4) if unit is None else (4 * self.half + 2 * unit, 2)
+        return self.x.at[at(self.half, f, s), pl.ds(lo, n)]
+
+    def push(self, f, s, unit, device, tf, ts, src=None):
+        self.mail.send(("g", self.half, tf % 4, ts % 4, unit), self.part(f, s, unit) if src is None else src,
+                       self.part(tf, ts, unit), device)
+
+    def got(self, f, s, unit):
+        self.mail.arrived(("g", self.half, f % 4, s % 4, unit), self.part(f, s, unit), self.fp)
+
+    def across(self, f):
+        self.push(f, 0, None, self.sp, f, 3)
+        self.push(f, 0, None, self.sm, f, 1)
+
+    def start(self):
+        self.push(0, 0, None, self.fp, 3, 0)
+        self.push(0, 0, None, self.fm, 1, 0)
+        self.across(0)
+
+    def first(self, f):
+        self.got(f, 0, None)
+        if f == 3:
+            self.push(3, 0, 0, self.fp, 2, 0)
+        else:
+            self.push(1, 0, 1, self.fm, 2, 0)
+        self.across(f)
+
+    def first_far(self):
+        self.got(2, 0, 0)
+        self.got(2, 0, 1)
+        self.across(2)
+
+    def second(self, f):
+        self.got(f, 3, None)
+        self.push(f, 3, 0, self.sp, f, 2)
+        self.got(f, 1, None)
+        self.push(f, 1, 1, self.sm, f, 2)
+
+    def second_far(self, f):
+        self.got(f, 2, 0)
+        self.got(f, 2, 1)
+
+
+class Reduce:
+    def __init__(self, mail, p, r1, r2, q1, q2, half, seq):
+        self.mail, self.p, self.half = mail, p, half
+        self.r1, self.r2, self.q1, self.q2 = r1, r2, q1, q2
+        self.fp, self.fm, self.sp, self.sm = ring(half, seq)
+
+    def unit(self, f, s, u):
+        return self.p.at[at(self.half, f, s), pl.ds(4 * self.half + 2 * u, 2)]
+
+    def push(self, key, src, dst, device):
+        self.mail.send((self.half,) + key, src, dst, device)
+
+    def got(self, key, dst):
+        self.mail.arrived((self.half,) + key, dst, self.fp)
+        return dst
+
+    def add(self, f, s, u, *others):
+        mine = self.unit(f, s, u)
+        for k in range(2):
+            total = mine[k].astype(jnp.float32)
+            for other in others:
+                total += other[k].astype(jnp.float32)
+            mine[k] = total.astype(jnp.bfloat16)
+
+    def start(self, f):
+        h = self.half
+        self.push(("r1", f, 0), self.unit(f, 2, 0), self.r1.at[h, f, 0], self.sp)
+        self.push(("r1", f, 1), self.unit(f, 2, 1), self.r1.at[h, f, 1], self.sm)
+        self.push(("r2", f, 0, 1), self.unit(f, 1, 1), self.r2.at[h, f, 0, 1], self.sp)
+        self.push(("r2", f, 1, 0), self.unit(f, 3, 0), self.r2.at[h, f, 1, 0], self.sm)
+
+    def middle(self, f):
+        h = self.half
+        self.add(f, 1, 0, self.got(("r1", f, 0), self.r1.at[h, f, 0]))
+        self.push(("r2", f, 0, 0), self.unit(f, 1, 0), self.r2.at[h, f, 0, 0], self.sp)
+        self.add(f, 3, 1, self.got(("r1", f, 1), self.r1.at[h, f, 1]))
+        self.push(("r2", f, 1, 1), self.unit(f, 3, 1), self.r2.at[h, f, 1, 1], self.sm)
+
+    def end(self, f):
+        h = self.half
+        for u in (0, 1):
+            self.add(f, 0, u, self.got(("r2", f, 0, u), self.r2.at[h, f, 0, u]),
+                     self.got(("r2", f, 1, u), self.r2.at[h, f, 1, u]))
+        if f == 2:
+            self.push(("q1", 0), self.unit(2, 0, 0), self.q1.at[h, 0], self.fp)
+            self.push(("q1", 1), self.unit(2, 0, 1), self.q1.at[h, 1], self.fm)
+        if f == 1:
+            self.push(("q2", 0, 1), self.unit(1, 0, 1), self.q2.at[h, 0, 1], self.fp)
+            self.add(1, 0, 0, self.got(("q1", 0), self.q1.at[h, 0]))
+            self.push(("q2", 0, 0), self.unit(1, 0, 0), self.q2.at[h, 0, 0], self.fp)
+        if f == 3:
+            self.push(("q2", 1, 0), self.unit(3, 0, 0), self.q2.at[h, 1, 0], self.fm)
+            self.add(3, 0, 1, self.got(("q1", 1), self.q1.at[h, 1]))
+            self.push(("q2", 1, 1), self.unit(3, 0, 1), self.q2.at[h, 1, 1], self.fm)
+
+    def last(self, u, out):
+        h = self.half
+        a = self.got(("q2", 0, u), self.q2.at[h, 0, u])
+        b = self.got(("q2", 1, u), self.q2.at[h, 1, u])
+        mine = self.unit(0, 0, u)
+        for k in range(2):
+            total = mine[k].astype(jnp.float32) + a[k].astype(jnp.float32) + b[k].astype(jnp.float32)
+            out[4 * h + 2 * u + k] = total.astype(out.dtype)
+
+
+def expert_kernel(x_in, wg_in, wu_in, wd_in, out, x, p, wg, wu, wd, acc_g, acc_u, act, r1, r2, q1, q2,
+                  load_sem, send_sem, recv_sem):
+    seq = lax.axis_index("seq")
+    loads = [pltpu.make_async_copy(wg_in, wg, load_sem.at[0]), pltpu.make_async_copy(wu_in, wu, load_sem.at[1])]
+    for k in range(SL):
+        loads.append(pltpu.make_async_copy(wd_in.at[:, pl.ds(k * W, W)], wd.at[k], load_sem.at[2 + k]))
+    own = pltpu.make_async_copy(x_in, x.at[0], load_sem.at[2 + SL])
+    own.start()
+    barrier = pltpu.get_barrier_semaphore()
+    for device in ring(0, seq):
+        pl.semaphore_signal(barrier, inc=1, device_id=device, device_id_type=MESH)
+    pl.semaphore_wait(barrier, 4)
+    own.wait()
+
+    mail = Mail(send_sem, recv_sem)
+    gathers = [Gather(mail, x, half, seq) for half in (0, 1)]
+    reduces = [Reduce(mail, p, r1, r2, q1, q2, half, seq) for half in (0, 1)]
+
+    def compute(group):
+        rows = pl.ds(4 * group, 4)
+        acc_g[...] = jnp.zeros_like(acc_g)
+        acc_u[...] = jnp.zeros_like(acc_u)
+
+        def up(k, _):
+            block = x[rows, k].astype(jnp.float32).reshape(4 * CAP, W).astype(jnp.bfloat16)
+            acc_g[...] += jnp.dot(block, wg[k], preferred_element_type=jnp.float32)
+            acc_u[...] += jnp.dot(block, wu[k], preferred_element_type=jnp.float32)
+            return 0
+
+        lax.fori_loop(0, SL, up, 0)
+        gate = acc_g[...]
+        act[...] = (gate / (1.0 + jnp.exp(-gate)) * acc_u[...]).astype(jnp.bfloat16)
+
+        def down(k, _):
+            block = jnp.dot(act[...], wd[k], preferred_element_type=jnp.float32)
+            p[rows, k] = block.reshape(4, CAP, W).astype(jnp.bfloat16)
+            return 0
+
+        lax.fori_loop(0, SL, down, 0)
+
+    for g in gathers:
+        g.start()
+    for copy in loads:
+        copy.start()
+    for f in (3, 1):
+        for g in gathers:
+            g.first(f)
+    for g in gathers:
+        g.second(0)
+    for copy in loads:
+        copy.wait()
+    compute(0)
+    for g in gathers:
+        g.first_far()
+    for f in (3, 1):
+        for g in gathers:
+            g.second(f)
+    compute(1)
+    for g in gathers:
+        g.second(2)
+    for g in gathers:
+        g.second_far(0)
+    for f in (3, 1):
+        for g in gathers:
+            g.second_far(f)
+    compute(2)
+    for g in gathers:
+        g.second_far(2)
+    compute(3)
+
+    def each(step, f):
+        for r in reduces:
+            getattr(r, step)(f)
+
+    each("start", 2)
+    each("start", 1)
+    each("middle", 2)
+    each("start", 3)
+    each("middle", 1)
+    each("end", 2)
+    each("start", 0)
+    each("middle", 3)
+    each("end", 1)
+    each("middle", 0)
+    each("end", 3)
+    each("end", 0)
+    for u in (0, 1):
+        for r in reduces:
+            r.last(u, out)
+    mail.drain()
+
+
+N_MAIL = 40 + 48 + 12
+
+
+def experts(x, w_gate, w_up, w_down):
+    vmem = pl.BlockSpec(memory_space=pltpu.VMEM)
+    hbm = pl.BlockSpec(memory_space=pl.ANY)
+    bf = jnp.bfloat16
+    return pl.pallas_call(
+        expert_kernel,
+        out_shape=jax.ShapeDtypeStruct((SL, CAP, W), bf),
+        in_specs=[vmem, hbm, hbm, hbm],
+        out_specs=vmem,
+        scratch_shapes=[
+            pltpu.VMEM((16, SL, CAP, W), bf),
+            pltpu.VMEM((16, SL, CAP, W), bf),
+            pltpu.VMEM((SL, W, F), bf),
+            pltpu.VMEM((SL, W, F), bf),
+            pltpu.VMEM((SL, F, W), bf),
+            pltpu.VMEM((4 * CAP, F), jnp.float32),
+            pltpu.VMEM((4 * CAP, F), jnp.float32),
+            pltpu.VMEM((4 * CAP, F), bf),
+            pltpu.VMEM((2, 4, 2, 2, CAP, W), bf),
+            pltpu.VMEM((2, 4, 2, 2, 2, CAP, W), bf),
+            pltpu.VMEM((2, 2, 2, CAP, W), bf),
+            pltpu.VMEM((2, 2, 2, 2, CAP, W), bf),
+            pltpu.SemaphoreType.DMA((3 + SL,)),
+            pltpu.SemaphoreType.DMA((N_MAIL,)),
+            pltpu.SemaphoreType.DMA((N_MAIL,)),
+        ],
+        compiler_params=pltpu.CompilerParams(collective_id=1, has_side_effects=True, vmem_limit_bytes=60 * 2**20),
+        name="experts",
+    )(x, w_gate.reshape(SL, W, F), w_up.reshape(SL, W, F), w_down)
 
 HS = 128
 
@@ -37,12 +324,6 @@
     first_doc = jnp.where(first_one >= 0, first_one, first_two)
     last_doc = jnp.where(last_two >= 0, last_two, last_one)
     return (through, head_state, first_doc, last_doc)
-
-
-def expert_act(row_block, w_gate, w_up):
-    gate_part = jnp.dot(row_block, w_gate[0], preferred_element_type=jnp.float32)
-    up_part = jnp.dot(row_block, w_up[0], preferred_element_type=jnp.float32)
-    return (jax.nn.silu(gate_part) * up_part).astype(jnp.bfloat16)
 
 
 def shards(
@@ -136,15 +417,8 @@
         * lax.rsqrt(jnp.mean(hidden_slots * hidden_slots, axis=-1, keepdims=True) + 1e-06)
         * norm_gain
     ).astype(jnp.bfloat16)
-    gathered = lax.all_gather(normed, "seq", axis=0, tiled=True)
-    row_block = gathered
-    act = expert_act(row_block, w_gate, w_up)
-    expert_out = lax.psum_scatter(
-        jnp.dot(act, w_down[0], preferred_element_type=jnp.float32).astype(jnp.bfloat16),
-        "seq",
-        scatter_dimension=0,
-        tiled=True,
-    ).astype(jnp.float32)
+    blocks = normed.reshape(capacity, SL, W).transpose(1, 0, 2)
+    expert_out = experts(blocks, w_gate[0], w_up[0], w_down[0]).transpose(1, 0, 2).reshape(capacity, SL * W)
     back_hidden, back_expert = (
         lax.all_to_all(
             hidden_slots.astype(jnp.bfloat16), "hx", split_axis=1, concat_axis=0, tiled=True

time: 450 us -> 327 us (0.73)
  waiting for transfers between devices: 271 us -> 98.2 us
  Pallas kernels: 0 us -> 97.2 us
  matrix products: 30.6 us -> 12 us
  other arithmetic: 27 us -> 9.13 us
  local copies, waits for them, and re-layouts: 42 us -> 27.5 us
    pallas_call x0 -> x1, Pallas kernels: none -> 97.2 us  [experts(): pl.pallas_call(expert_kernel, out_shape=jax.ShapeDtypeStruct((SL, CAP, W)...]
    unnamed x5 -> x2, waiting for transfers between devices: 74.3 us -> 0.03 us
    all_gather x1 -> x0, waiting for transfers between devices: 70.5 us -> none  [shards(): gathered = lax.all_gather(normed, 'seq', axis=0, tiled=True)]
    reduce_scatter x1, waiting for transfers between devices: 123 us -> 90 us  [shards(): lax.psum_scatter(jnp.dot(row_block, out_weight, preferred_element_type=jn...]
    dot_general x3 -> x0, matrix products: 16.7 us -> none  [the longest x1 7.31 us: expert_act(): jnp.dot(row_block, w_gate[0], preferred_element_type=jnp.float32)]
    unnamed x21 -> x17, local copies, waits for them, and re-layouts: 7.71 us -> 18 us
    all_to_all x1, waiting for transfers between devices: 3.47 us -> 8.19 us  [shards(): lax.all_to_all(expert_out.astype(jnp.bfloat16), 'hx', split_axis=1, conca...]
  transfers between devices with their start and end apart: 6 -> 4, of which waited for: 4 -> 2; matrix products, arithmetic and copies ran while one was open for 8% -> 8% of each run, Pallas kernels for 0% -> 30%
where the time goes in v1:
time: 327 us; the launch traced here: 325 us
  waiting for transfers between devices  98.2 us (30%)
  Pallas kernels  97.2 us (30%)
  blocking collectives  49.5 us (15%)
  local copies, waits for them, and re-layouts  27.5 us (8%)
  starting transfers between devices  15.8 us (5%)
  between operations  15.5 us (5%)
  matrix products  12 us (4%)
  other arithmetic  9.13 us (3%)
    pallas_call x1, Pallas kernels, experts(): pl.pallas_call(expert_kernel, out_shape=jax.ShapeDtypeStruct((SL, CAP, W)...  97.2 us
    reduce_scatter x1, waiting for transfers between devices, shards(): lax.psum_scatter(jnp.dot(row_block, out_weight, preferred_element_type=jn...  90 us
    unnamed x1, blocking collectives  35.8 us
    unnamed x17, local copies, waits for them, and re-layouts  18 us
    all_gather x1, blocking collectives, prefix(): lax.all_gather(a.astype(kind), axis)  13.7 us
    all_to_all x1, starting transfers between devices, shards(): lax.all_to_all(expert_out.astype(jnp.bfloat16), 'hx', split_axis=1, conca...  8.68 us
    all_to_all x1, waiting for transfers between devices, shards(): lax.all_to_all(expert_out.astype(jnp.bfloat16), 'hx', split_axis=1, conca...  8.19 us
    all_to_all x1, starting transfers between devices, shards(): lax.all_to_all(hidden_slots.astype(jnp.bfloat16), 'hx', split_axis=1, con...  7.09 us
  transfers between devices with their start and end apart: 4, of which 2 were waited for; matrix products, arithmetic and copies ran while one was open for 8% of the time, Pallas kernels for 30%

profile of v1, /device:TPU:1, one launch (start us, length us, event | category | flops | bytes accessed | tf_op | source)
XLA Modules:
  0.0 324.9 jit_solution(18431907162077526527)
XLA Ops:
  6.5 0.0 copy-start
  6.5 0.0 all-gather.6.cloned.1.call-start
  6.5 1.4 fusion.29
  9.2 1.9 compare_convert_fusion
  11.1 0.8 copy.74
  11.9 0.2 reduce_window_sum.28
  12.1 0.1 exponential_multiply_fusion
  12.2 0.1 copy.80
  12.3 1.0 copy.92
  13.3 1.8 convolution_convert_fusion.1
  15.1 0.0 all-gather.6.cloned.1.call-update
  15.2 0.0 reduce-scatter.2.cloned.1.call-start
  15.2 1.2 dynamic-slice
  16.4 1.3 dynamic-update-slice
  17.7 1.3 dynamic-update-slice.1
  19.0 35.8 %all-reduce.2 = (bf16[16]{0:T(256)(128)(2,1)S(1)}, bf16[16]{0:T(256)(128)(2,1)S(1)}) all-reduce(bf16[16]{0:T(256)(128)(2,1)S(1)} %dynamic-update-slice, bf16[16]{0:T(256)(128)(2,1)S(1)} %dynamic-update-slice.1), channel_id=2, replica_groups=mesh['seq'=16,'hx'=8] {'seq'}, use_global_device_ids=true, to_apply=%add | all-reduce | flops 32 | bytes 128
  54.8 13.7 %all-gather.3 = bf16[16,1,4]{2,1,0:T(2,128)(2,1)S(1)} all-gather(bf16[1,1,4]{2,1,0:T(2,128)(2,1)S(1)} %get-tuple-element.132), channel_id=1, replica_groups=mesh['seq'=16,'hx'=8] {'seq'}, dimensions={0}, use_global_device_ids=true | all-gather | bytes 136 | tf_op jit(solution)/shard_map/all_gather | solution.py:299
  69.1 0.8 copy.70
  69.9 0.1 reshape.214
  70.0 0.1 eq.79
  70.2 0.6 reduce-window.6
  70.8 0.2 slice_reduce_fusion
  71.0 0.1 copy.75
  71.1 0.1 copy.78
  71.2 0.1 copy.82
  71.3 0.1 fusion.25
  71.4 0.1 select_reduce_fusion
  71.6 0.1 fusion.6
  71.7 0.8 fusion.23
  72.6 1.1 convolution_multiply_fusion
  73.7 1.3 convolution_bitcast_fusion.1
  75.0 0.0 all-gather.6.cloned.1.call-done
  75.1 0.1 multiply_multiply_fusion
  75.2 0.1 copy.84
  75.2 0.0 copy-done.1
  75.2 0.7 multiply_reduce_fusion.1
  76.0 0.1 copy.86
  76.1 2.0 gather_fusion.1
  78.1 7.0 %convolution_convert_fusion = bf16[320,6144]{1,0:T(8,128)(2,1)} fusion(bf16[512,6144]{1,0:T(8,128)(2,1)} %param.21, bf16[320,512]{1,0:T(8,128)(2,1)S(1)} %gather_fusion.1, pred[320]{0:T(512)(128)(4,1)S(1)} %fusion.6), kind=kOutput, calls=%fused_computation.12 | convolution fusion | flops 2015395840 | bytes 10551616 | tf_op jit(solution)/shard_map/dot_general | solution.py:408
  85.1 0.0 reduce-scatter.2.cloned.1.call-update
  85.2 0.2 slice.36
  85.4 0.2 slice.33
  85.6 6.3 %copy.89 = bf16[1,6144,288]{2,1,0:T(8,128)(2,1)} copy(bf16[1,6144,288]{1,2,0:T(8,128)(2,1)} %param.25) | data formatting | bytes 7077888 | tf_op args[10]
  91.9 6.4 %copy.90 = bf16[1,6144,288]{2,1,0:T(8,128)(2,1)} copy(bf16[1,6144,288]{1,2,0:T(8,128)(2,1)} %param.26) | data formatting | bytes 7077888 | tf_op args[11]
  98.2 0.1 compare_select_fusion.3
  98.3 0.0 copy-done
  98.3 0.0 copy-start.2
  98.3 0.8 gather_fusion
  99.2 90.0 %reduce-scatter.2.cloned.1.call-done = bf16[40,6144]{1,0:T(8,128)(2,1)} async-done(((bf16[320,6144]{1,0:T(8,128)(2,1)}), bf16[40,6144]{1,0:T(8,128)(2,1)}) %reduce-scatter.2.cloned.1.call-update) | async-done | bytes 491536 | tf_op jit(solution)/shard_map/reduce_scatter | solution.py:407
  189.2 1.3 fusion.4
  190.5 0.8 copy.118
  191.3 7.1 %all-to-all-start = ((bf16[40,8,768]{2,0,1:T(8,128)(2,1)}), bf16[40,8,768]{2,0,1:T(8,128)(2,1)S(1)}, u32[]{:S(2)}, u32[]{:S(2)}) async-start(bf16[40,8,768]{2,0,1:T(8,128)(2,1)} %bitcast.95), calls=%async_computation.1 | async-start | bytes 983040 | tf_op jit(solution)/shard_map/all_to_all | solution.py:423
  198.4 0.0 copy-done.2
  198.4 1.2 multiply_convert_fusion
  199.6 0.8 copy.117
  200.5 97.2 %experts.1 = bf16[8,40,768]{2,1,0:T(8,128)(2,1)} custom-call(bf16[8,40,768]{2,1,0:T(8,128)(2,1)} %bitcast.115, bf16[8,768,288]{2,1,0:T(8,128)(2,1)} %bitcast.108, bf16[8,768,288]{2,1,0:T(8,128)(2,1)} %bitcast.109, bf16[288,6144]{1,0:T(8,128)(2,1)} %bitcast.111), custom_call_target="tpu_custom_call" | custom-call | tf_op jit(solution)/shard_map/experts/pallas_call | solution.py:267
  297.7 0.0 all-to-all-done
  297.7 8.7 %all-to-all-start.1 = ((bf16[40,8,768]{2,0,1:T(8,128)(2,1)}), bf16[40,8,768]{2,0,1:T(8,128)(2,1)S(1)}, u32[]{:S(2)}, u32[]{:S(2)}) async-start(bf16[40,8,768]{2,0,1:T(8,128)(2,1)} %bitcast.114), calls=%async_computation.2 | async-start | bytes 983040 | tf_op jit(solution)/shard_map/all_to_all | solution.py:426
  306.4 0.1 convert_element_type.152
  306.5 0.8 gather_fusion.2
  307.3 8.2 %all-to-all-done.1 = bf16[40,8,768]{2,0,1:T(8,128)(2,1)S(1)} async-done(((bf16[40,8,768]{2,0,1:T(8,128)(2,1)}), bf16[40,8,768]{2,0,1:T(8,128)(2,1)S(1)}, u32[]{:S(2)}, u32[]{:S(2)}) %all-to-all-start.1) | async-done | bytes 491552 | tf_op jit(solution)/shard_map/all_to_all | solution.py:426
  315.5 0.9 gather_fusion.3
  316.3 0.9 gather_fusion.4
  317.2 0.8 add_convert_fusion
  (23 shorter events, 0.2 us)
Async XLA Ops:
  6.5 91.8 %copy-start = (bf16[128,6144]{1,0:T(8,128)(2,1)S(1)}, bf16[128,6144]{1,0:T(8,128)(2,1)}, u32[]{:S(2)}) copy-start(bf16[128,6144]{1,0:T(8,128)(2,1)} %param.20) | copy-start | bytes 4718596
  6.5 68.7 %copy-start.1 = (bf16[128,512]{1,0:T(8,128)(2,1)S(1)}, bf16[128,512]{1,0:T(8,128)(2,1)}, u32[]{:S(2)}) copy-start(bf16[128,512]{1,0:T(8,128)(2,1)} %param.15) | copy-start | bytes 393220
  6.5 68.5 %all-gather.6.cloned.1.call-start = ((), (), s32[]{:S(2)}) async-start(), calls=%async_computation.4 | async-start | bytes 2228224 | tf_op jit(solution)/shard_map/all_gather | solution.py:299
  15.2 174.0 %reduce-scatter.2.cloned.1.call-start = ((), (), s32[]{:S(2)}) async-start(), calls=%async_computation.3 | async-start | bytes 4423680 | tf_op jit(solution)/shard_map/reduce_scatter | solution.py:407
  98.3 100.1 %copy-start.2 = (f32[6144]{0:T(1024)S(1)}, f32[6144]{0:T(1024)}, u32[]{:S(2)}) copy-start(f32[6144]{0:T(1024)} %param.22) | copy-start | bytes 73732
  191.3 106.3 %all-to-all-start = ((bf16[40,8,768]{2,0,1:T(8,128)(2,1)}), bf16[40,8,768]{2,0,1:T(8,128)(2,1)S(1)}, u32[]{:S(2)}, u32[]{:S(2)}) async-start(bf16[40,8,768]{2,0,1:T(8,128)(2,1)} %bitcast.95), calls=%async_computation.1 | async-start | bytes 983040 | tf_op jit(solution)/shard_map/all_to_all | solution.py:423
  200.5 105.9 %copy-start.3 = (f32[128,2]{0,1:T(2,128)S(1)}, f32[128,2]{0,1:T(2,128)}, u32[]{:S(2)}) copy-start(f32[128,2]{0,1:T(2,128)} %param.24) | copy-start | bytes 3076
  297.7 17.8 %all-to-all-start.1 = ((bf16[40,8,768]{2,0,1:T(8,128)(2,1)}), bf16[40,8,768]{2,0,1:T(8,128)(2,1)S(1)}, u32[]{:S(2)}, u32[]{:S(2)}) async-start(bf16[40,8,768]{2,0,1:T(8,128)(2,1)} %bitcast.114), calls=%async_computation.2 | async-start | bytes 983040 | tf_op jit(solution)/shard_map/all_to_all | solution.py:426
Sparse Core Ops, SparseCore 0:
  15.3 47.4 all-gather.5
  85.3 103.8 reduce-scatter.1

commit v2 on v1

v2 whole, which is shorter than its diff:
```python
import jax
import jax.numpy as jnp
from jax import lax
from jax.experimental import pallas as pl
from jax.experimental.pallas import tpu as pltpu
from jax.sharding import PartitionSpec as P

MESH = pl.DeviceIdType.MESH
CAP = 40
HS = 128
HEADS = 4
T = 128
N_SEQ = 16
SL = 8
W = 768
F = 288
ORDER = [(0, 0), (1, 0), (3, 0), (0, 1), (0, 3), (1, 1), (1, 3), (3, 1), (3, 3), (2, 0), (0, 2), (1, 2), (3, 2), (2, 1), (2, 3), (2, 2)]
SLOT = {r: i for i, r in enumerate(ORDER)}


def at(half, first, second):
    return SLOT[(first % 4, second % 4) if half == 0 else (second % 4, first % 4)]


class Mail:
    def __init__(self, send_sem, recv_sem):
        self.send_sem, self.recv_sem = send_sem, recv_sem
        self.number, self.sent = {}, []

    def make(self, key, src, dst, device):
        n = self.number.setdefault(key, len(self.number))
        return pltpu.make_async_remote_copy(
            src_ref=src, dst_ref=dst, send_sem=self.send_sem.at[n], recv_sem=self.recv_sem.at[n],
            device_id=device, device_id_type=MESH)

    def send(self, key, src, dst, device):
        copy = self.make(key, src, dst, device)
        copy.start()
        self.sent.append(copy)

    def arrived(self, key, dst, device):
        self.make(key, dst, dst, device).wait_recv()

    def drain(self):
        for copy in self.sent:
            copy.wait_send()


def ring(half, seq):
    y, z = seq // 4, seq % 4
    yp, ym = ((y + 1) % 4) * 4 + z, ((y + 3) % 4) * 4 + z
    zp, zm = y * 4 + (z + 1) % 4, y * 4 + (z + 3) % 4
    ids = (yp, ym, zp, zm) if half == 0 else (zp, zm, yp, ym)
    return [{"seq": i} for i in ids]


class Gather:
    def __init__(self, mail, x, half, seq):
        self.mail, self.x, self.half = mail, x, half
        self.fp, self.fm, self.sp, self.sm = ring(half, seq)

    def part(self, f, s, unit):
        lo, n = (4 * self.half, 4) if unit is None else (4 * self.half + 2 * unit, 2)
        return self.x.at[at(self.half, f, s), pl.ds(lo, n)]

    def push(self, f, s, unit, device, tf, ts, src=None):
        self.mail.send(("g", self.half, tf % 4, ts % 4, unit), self.part(f, s, unit) if src is None else src,
                       self.part(tf, ts, unit), device)

    def got(self, f, s, unit):
        self.mail.arrived(("g", self.half, f % 4, s % 4, unit), self.part(f, s, unit), self.fp)

    def across(self, f):
        self.push(f, 0, None, self.sp, f, 3)
        self.push(f, 0, None, self.sm, f, 1)

    def start(self):
        self.push(0, 0, None, self.fp, 3, 0)
        self.push(0, 0, None, self.fm, 1, 0)
        self.across(0)

    def first(self, f):
        self.got(f, 0, None)
        if f == 3:
            self.push(3, 0, 0, self.fp, 2, 0)
        else:
            self.push(1, 0, 1, self.fm, 2, 0)
        self.across(f)

    def first_far(self):
        self.got(2, 0, 0)
        self.got(2, 0, 1)
        self.across(2)

    def second(self, f):
        self.got(f, 3, None)
        self.push(f, 3, 0, self.sp, f, 2)
        self.got(f, 1, None)
        self.push(f, 1, 1, self.sm, f, 2)

    def second_far(self, f):
        self.got(f, 2, 0)
        self.got(f, 2, 1)


class Reduce:
    def __init__(self, mail, p, r1, r2, q1, q2, half, seq):
        self.mail, self.p, self.half = mail, p, half
        self.r1, self.r2, self.q1, self.q2 = r1, r2, q1, q2
        self.fp, self.fm, self.sp, self.sm = ring(half, seq)

    def unit(self, f, s, u):
        return self.p.at[at(self.half, f, s), pl.ds(4 * self.half + 2 * u, 2)]

    def push(self, key, src, dst, device):
        self.mail.send((self.half,) + key, src, dst, device)

    def got(self, key, dst):
        self.mail.arrived((self.half,) + key, dst, self.fp)
        return dst

    def add(self, f, s, u, *others):
        mine = self.unit(f, s, u)
        for k in range(2):
            total = mine[k].astype(jnp.float32)
            for other in others:
                total += other[k].astype(jnp.float32)
            mine[k] = total.astype(jnp.bfloat16)

    def start(self, f):
        h = self.half
        self.push(("r1", f, 0), self.unit(f, 2, 0), self.r1.at[h, f, 0], self.sp)
        self.push(("r1", f, 1), self.unit(f, 2, 1), self.r1.at[h, f, 1], self.sm)
        self.push(("r2", f, 0, 1), self.unit(f, 1, 1), self.r2.at[h, f, 0, 1], self.sp)
        self.push(("r2", f, 1, 0), self.unit(f, 3, 0), self.r2.at[h, f, 1, 0], self.sm)

    def middle(self, f):
        h = self.half
        self.add(f, 1, 0, self.got(("r1", f, 0), self.r1.at[h, f, 0]))
        self.push(("r2", f, 0, 0), self.unit(f, 1, 0), self.r2.at[h, f, 0, 0], self.sp)
        self.add(f, 3, 1, self.got(("r1", f, 1), self.r1.at[h, f, 1]))
        self.push(("r2", f, 1, 1), self.unit(f, 3, 1), self.r2.at[h, f, 1, 1], self.sm)

    def end(self, f):
        h = self.half
        for u in (0, 1):
            self.add(f, 0, u, self.got(("r2", f, 0, u), self.r2.at[h, f, 0, u]),
                     self.got(("r2", f, 1, u), self.r2.at[h, f, 1, u]))
        if f == 2:
            self.push(("q1", 0), self.unit(2, 0, 0), self.q1.at[h, 0], self.fp)
            self.push(("q1", 1), self.unit(2, 0, 1), self.q1.at[h, 1], self.fm)
        if f == 1:
            self.push(("q2", 0, 1), self.unit(1, 0, 1), self.q2.at[h, 0, 1], self.fp)
            self.add(1, 0, 0, self.got(("q1", 0), self.q1.at[h, 0]))
            self.push(("q2", 0, 0), self.unit(1, 0, 0), self.q2.at[h, 0, 0], self.fp)
        if f == 3:
            self.push(("q2", 1, 0), self.unit(3, 0, 0), self.q2.at[h, 1, 0], self.fm)
            self.add(3, 0, 1, self.got(("q1", 1), self.q1.at[h, 1]))
            self.push(("q2", 1, 1), self.unit(3, 0, 1), self.q2.at[h, 1, 1], self.fm)

    def last(self, u, out):
        h = self.half
        a = self.got(("q2", 0, u), self.q2.at[h, 0, u])
        b = self.got(("q2", 1, u), self.q2.at[h, 1, u])
        mine = self.unit(0, 0, u)
        for k in range(2):
            total = mine[k].astype(jnp.float32) + a[k].astype(jnp.float32) + b[k].astype(jnp.float32)
            out[4 * h + 2 * u + k] = total.astype(out.dtype)


def iota(shape, dim):
    return lax.broadcasted_iota(jnp.int32, shape, dim)


def f32(a):
    return a.astype(jnp.float32)


def bf16(a):
    return a.astype(jnp.bfloat16)


def dot(a, b, ca=1, cb=0, **kw):
    return lax.dot_general(a, b, (((ca,), (cb,)), ((), ())), preferred_element_type=jnp.float32, **kw)


def dispatch(ids):
    experts = iota((SL, T), 0)
    named = (ids[0:1, :] == experts) | (ids[1:2, :] == experts)
    before = bf16(jnp.where(iota((T, T), 0) < iota((T, T), 1), 1.0, 0.0))
    rank = dot(bf16(jnp.where(named, 1.0, 0.0)), before)
    slot = f32(iota((CAP, T), 0))
    chosen = f32(jnp.where(named, 1.0, 0.0))
    return [jnp.where(rank[e : e + 1, :] == slot, 1.0, 0.0) * chosen[e : e + 1, :] for e in range(SL)]


def greet(seq, x, c):
    others = [{"seq": (seq + d) % N_SEQ} for d in range(1, N_SEQ)]
    others += [{"hx": (2 * x + c + d) % SL} for d in range(1, SL)]
    barrier = pltpu.get_barrier_semaphore()
    for device in others:
        pl.semaphore_signal(barrier, inc=1, device_id=device, device_id_type=MESH)
    pl.semaphore_wait(barrier, len(others))


def local_attention(q, k, v, decay, docs, states, head_out, carry):
    doc_row = jnp.broadcast_to(f32(docs[...]), (T, T))
    doc_col = doc_row.T
    allowed = (iota((T, T), 0) >= iota((T, T), 1)) & (doc_row == doc_col)
    upto = f32(jnp.where(iota((T, T), 0) <= iota((T, T), 1), 1.0, 0.0))
    rows = jnp.concatenate([decay[...], jnp.zeros((8 - HEADS, T), jnp.float32)], axis=0)
    sums = dot(rows, upto, precision=lax.Precision.HIGHEST)
    first, last = doc_col[0:1, :], doc_col[T - 1 : T, :]
    row = iota((16, HS), 0)
    for h in range(HEADS):
        lanes = slice(h * HS, (h + 1) * HS)
        across = jnp.broadcast_to(sums[h : h + 1, :], (T, T))
        down = across.T
        fade = jnp.where(allowed, jnp.exp(jnp.where(allowed, down - across, 0.0)), 0.0)
        scores = dot(q[:, lanes], k[:, lanes], 1, 1)
        head_out[h] = dot(bf16(scores * fade), v[:, lanes])
        total = down[T - 1 : T, :]
        to_end = jnp.where(doc_col == last, jnp.exp(total - down), 0.0)
        state = bf16(dot(bf16(f32(k[:, lanes]) * to_end), v[:, lanes], 0, 0))
        carry[h] = bf16(f32(q[:, lanes]) * jnp.where(doc_col == first, jnp.exp(down), 0.0))
        high = f32(bf16(total))
        mid = f32(bf16(total - high))
        low = total - high - mid
        facts = jnp.where(row == 0, high, jnp.where(row == 1, mid, jnp.where(row == 2, low, jnp.where(row == 3, first, last))))
        for part in range(4):
            states[4 * h + part, 0:32] = state[32 * part : 32 * (part + 1)]
            states[4 * h + part, 32:48] = bf16(facts)


def carry_states(mail, seq, states, arrived, entering, incoming, meanwhile):
    for d in range(1, N_SEQ):
        mail.send(("s", d), states.at[(seq + d) % N_SEQ], arrived.at[seq], {"seq": (seq + d) % N_SEQ})
    arrived[seq] = states[seq]
    meanwhile()
    for d in range(1, N_SEQ):
        mail.arrived(("s", d), arrived.at[(seq + N_SEQ - d) % N_SEQ], {"seq": (seq + d) % N_SEQ})
    state = jnp.zeros((32, HS), jnp.float32)
    before = jnp.full((1, HS), -1.0, jnp.float32)
    for s in range(N_SEQ):
        facts = f32(arrived[s, 32:48])
        log_total = facts[0:1] + facts[1:2] + facts[2:3]
        first, last = facts[3:4], facts[4:5]
        state = state * jnp.where(before == first, 1.0, 0.0)
        entering[s] = bf16(state)
        state = state * jnp.where(first == last, jnp.exp(log_total), 0.0) + f32(arrived[s, 0:32])
        before = last
    for d in range(1, N_SEQ):
        mail.send(("c", d), entering.at[(seq + d) % N_SEQ], incoming.at[seq], {"seq": (seq + d) % N_SEQ})
    incoming[seq] = entering[seq]
    for d in range(1, N_SEQ):
        mail.arrived(("c", d), incoming.at[(seq + N_SEQ - d) % N_SEQ], {"seq": (seq + d) % N_SEQ})


def attention_rows(head_out, carry, incoming, attn):
    for h in range(HEADS):
        state = incoming[4 * h : 4 * h + 4].reshape(HS, HS)
        out = head_out[h] + dot(carry[h], state)
        mean = jnp.mean(out * out, axis=1, keepdims=True)
        attn[:, h * HS : (h + 1) * HS] = bf16(out * lax.rsqrt(mean + 1e-05))


HALF = T // 2


def project(mail, x, c, attn, wo, to_twin, from_twin, part, r1, r2, residual, hidden):
    twin = {"hx": 2 * x + 1 - c}
    up, down = {"hx": 2 * ((x + 1) % 4) + c}, {"hx": 2 * ((x + 3) % 4) + c}
    order = (2, 1, 3, 0)

    def send_twin(dx):
        to_twin[dx] = bf16(dot(attn[...], wo[2 * dx + 1 - c])).reshape(2, HALF, W)
        mail.send(("t", dx), to_twin.at[dx], from_twin.at[dx], twin)

    def both(dx):
        mine = dot(attn[...], wo[2 * dx + c]).reshape(2, HALF, W)
        mail.arrived(("t", dx), from_twin.at[dx], twin)
        return mine + f32(from_twin[dx])

    send_twin(2)
    send_twin(1)
    part[2] = bf16(both(2))
    mail.send(("p1", 0), part.at[2, 0], r1.at[0], up)
    mail.send(("p1", 1), part.at[2, 1], r1.at[1], down)
    send_twin(3)
    mine = both(1)
    part[1, 1] = bf16(mine[1])
    mail.send(("p2", 0, 1), part.at[1, 1], r2.at[0, 1], up)
    send_twin(0)
    mail.arrived(("p1", 0), r1.at[0], up)
    part[1, 0] = bf16(mine[0] + f32(r1[0]))
    mail.send(("p2", 0, 0), part.at[1, 0], r2.at[0, 0], up)
    mine = both(3)
    part[3, 0] = bf16(mine[0])
    mail.send(("p2", 1, 0), part.at[3, 0], r2.at[1, 0], down)
    mail.arrived(("p1", 1), r1.at[1], up)
    part[3, 1] = bf16(mine[1] + f32(r1[1]))
    mail.send(("p2", 1, 1), part.at[3, 1], r2.at[1, 1], down)
    mine = both(0)
    for u in (1, 0):
        rows = slice(u * HALF, (u + 1) * HALF)
        mail.arrived(("p2", 0, u), r2.at[0, u], up)
        mail.arrived(("p2", 1, u), r2.at[1, u], up)
        hidden[rows, :] = f32(residual[rows, :]) + mine[u] + f32(r2[0, u]) + f32(r2[1, u])


WS = W + 128


class Cross:
    def __init__(self, send_sem, recv_sem, x, c):
        self.send_sem, self.recv_sem, self.x, self.c, self.sent = send_sem, recv_sem, x, c, []

    def make(self, dx, to, own, src, dst):
        return pltpu.make_async_remote_copy(
            src_ref=src, dst_ref=dst, send_sem=self.send_sem.at[2 * dx + to], recv_sem=self.recv_sem.at[2 * dx + own],
            device_id={"hx": 2 * ((self.x + dx) % 4) + to}, device_id_type=MESH)

    def send(self, dx, to, src, dst):
        copy = self.make(dx, to, self.c, src, dst)
        copy.start()
        self.sent.append(copy)

    def arrived(self, dx, own, dst):
        self.make(dx, own, own, dst, dst).wait_recv()

    def drain(self):
        for copy in self.sent:
            copy.wait_send()


def rows_to_experts(cross, x, c, hidden, pick, out, slots):
    square = jnp.sum(hidden[...] * hidden[...], axis=1, keepdims=True)
    high = f32(bf16(square))
    facts = jnp.where(iota((T, 128), 1) < 64, high, square - high)
    rows = jnp.concatenate([bf16(hidden[...]), bf16(facts)], axis=1)
    for dx in (2, 1, 3):
        for to in (0, 1):
            out[2 * dx + to] = bf16(dot(pick[2 * ((x + dx) % 4) + to], rows))
            cross.send(dx, to, out.at[2 * dx + to], slots.at[2 * (4 - dx) + c])
    out[0] = bf16(dot(pick[2 * x + 1 - c], rows))
    cross.send(0, 1 - c, out.at[0], slots.at[c])
    slots[c] = bf16(dot(pick[2 * x + c], rows))
    cross.arrived(0, 1 - c, slots.at[1 - c])
    for dx in (1, 3, 2):
        for own in (0, 1):
            cross.arrived(dx, own, slots.at[2 * (4 - dx) + own])


def norm_rows(x, slots, gain, rows):
    square = sum(f32(slots[k, :, W:WS]) for k in range(SL))
    mean = (square[:, 0:1] + square[:, 64:65]) * (1.0 / (SL * W))
    scale = lax.rsqrt(mean + 1e-06)
    for k in range(SL):
        rows[0, k] = bf16(f32(slots[k, :, 0:W]) * scale * gain[pl.ds((2 * x + k) % SL, 1), :])


def run_experts(mail, seq, rows, p, wg, wu, wd, acc_g, acc_u, act, r1, r2, q1, q2, loads, out, finish):
    gathers = [Gather(mail, rows, half, seq) for half in (0, 1)]
    reduces = [Reduce(mail, p, r1, r2, q1, q2, half, seq) for half in (0, 1)]

    def compute(group):
        blocks = pl.ds(4 * group, 4)
        acc_g[...] = jnp.zeros_like(acc_g)
        acc_u[...] = jnp.zeros_like(acc_u)

        def up(k, _):
            block = bf16(f32(rows[blocks, k]).reshape(4 * CAP, W))
            acc_g[...] += dot(block, wg[k], 1, 1)
            acc_u[...] += dot(block, wu[k], 1, 1)
            return 0

        lax.fori_loop(0, SL, up, 0)
        gate = acc_g[...]
        act[...] = bf16(gate / (1.0 + jnp.exp(-gate)) * acc_u[...])

        def down(k, _):
            p[blocks, k] = bf16(dot(act[...], wd[k]).reshape(4, CAP, W))
            return 0

        lax.fori_loop(0, SL, down, 0)

    for g in gathers:
        g.start()
    for f in (3, 1):
        for g in gathers:
            g.first(f)
    for g in gathers:
        g.second(0)
    for copy in loads:
        copy.wait()
    compute(0)
    for g in gathers:
        g.first_far()
    for f in (3, 1):
        for g in gathers:
            g.second(f)
    compute(1)
    for g in gathers:
        g.second(2)
    for g in gathers:
        g.second_far(0)
    for f in (3, 1):
        for g in gathers:
            g.second_far(f)
    compute(2)
    for g in gathers:
        g.second_far(2)
    compute(3)

    def each(step, f):
        for r in reduces:
            getattr(r, step)(f)

    each("start", 2)
    each("start", 1)
    each("middle", 2)
    each("start", 3)
    each("middle", 1)
    each("end", 2)
    each("start", 0)
    each("middle", 3)
    each("end", 1)
    each("middle", 0)
    each("end", 3)
    each("end", 0)
    for u in (1, 0):
        for half in (1, 0):
            reduces[half].last(u, out)
            finish(2 * half + u)


def layer_kernel(q, k, v, decay, docs, residual_in, wo_in, gain, ids, weights, wg_in, wu_in, wd_in, result,
                 wo, residual, pick, states, arrived, entering, incoming, head_out, carry, attn,
                 to_twin, from_twin, part, s1, s2, hidden, slot_out, slots,
                 rows, p, wg, wu, wd, acc_g, acc_u, act, r1, r2, q1, q2, done, back,
                 load_sem, send_sem, recv_sem, out_send, out_recv, back_send, back_recv):
    seq, hx = lax.axis_index("seq"), lax.axis_index("hx")
    x, c = hx // 2, hx % 2

    def lanes(n):
        return pl.ds(pl.multiple_of(n * W, W), W)

    front = [pltpu.make_async_copy(wo_in.at[:, lanes((2 * x + n) % SL)], wo.at[n], load_sem.at[n]) for n in range(SL)]
    front.append(pltpu.make_async_copy(residual_in.at[:, lanes(hx)], residual, load_sem.at[SL]))
    loads = []
    for n in range(SL):
        here = lanes((2 * x + n) % SL)
        for j, (source, target) in enumerate(((wg_in, wg), (wu_in, wu), (wd_in, wd))):
            loads.append(pltpu.make_async_copy(source.at[:, here], target.at[n], load_sem.at[SL + 1 + 3 * n + j]))
    greet(seq, x, c)
    for copy in front:
        copy.start()
    for copy in loads:
        copy.start()

    mail = Mail(send_sem, recv_sem)
    local_attention(q, k, v, decay, docs, states, head_out, carry)
    carry_states(mail, seq, states, arrived, entering, incoming, lambda: fill_pick(ids, pick))
    attention_rows(head_out, carry, incoming, attn)
    for copy in front:
        copy.wait()
    project(mail, x, c, attn, wo, to_twin, from_twin, part, s1, s2, residual, hidden)
    out = Cross(out_send, out_recv, x, c)
    rows_to_experts(out, x, c, hidden, pick, slot_out, slots)
    norm_rows(x, slots, gain, rows)

    home = Cross(back_send, back_recv, x, c)

    def finish(dx):
        if dx == 0:
            home.send(0, 1 - c, done.at[1 - c], back.at[hx])
            back[hx] = done[c]
        else:
            for to in (0, 1):
                home.send(dx, to, done.at[2 * dx + to], back.at[hx])

    run_experts(mail, seq, rows, p, wg, wu, wd, acc_g, acc_u, act, r1, r2, q1, q2, loads, done, finish)

    weighted = []
    for e in range(SL):
        own = jnp.where(ids[0:1, :] == e, weights[0:1, :], 0.0) + jnp.where(ids[1:2, :] == e, weights[1:2, :], 0.0)
        weighted.append(f32(pick[e]) * own)
    weighted = jnp.concatenate(weighted, axis=0)
    high = bf16(weighted)
    low = bf16(weighted - f32(high))
    home.arrived(0, 1 - c, back.at[2 * x + 1 - c])
    for dx in (3, 1, 2):
        for own in (0, 1):
            home.arrived(dx, own, back.at[2 * ((x + 4 - dx) % 4) + own])
    expert_out = bf16(f32(back[...]).reshape(SL * CAP, W))
    result[...] = bf16(hidden[...] + dot(high, expert_out, 0, 0) + dot(low, expert_out, 0, 0))
    mail.drain()
    out.drain()
    home.drain()


def fill_pick(ids, pick):
    for e, block in enumerate(dispatch(ids)):
        pick[e] = bf16(block)


N_MAIL = 30 + 4 + 6 + 40 + 48 + 12


def shards(queries, keys, values, log_decay, doc_ids, residual, out_weight, norm_gain, expert_ids, route_weight, w_gate, w_up, w_down):
    vmem = pl.BlockSpec(memory_space=pltpu.VMEM)
    hbm = pl.BlockSpec(memory_space=pl.ANY)
    bf, fl = jnp.bfloat16, jnp.float32
    dma = pltpu.SemaphoreType.DMA
    scratch = [
        ((SL, HEADS * HS, W), bf), ((T, W), bf), ((SL, CAP, T), bf),
        ((N_SEQ, 48, HS), bf), ((N_SEQ, 48, HS), bf), ((N_SEQ, 32, HS), bf), ((N_SEQ, 32, HS), bf),
        ((HEADS, T, HS), fl), ((HEADS, T, HS), bf), ((T, HEADS * HS), bf),
        ((4, 2, HALF, W), bf), ((4, 2, HALF, W), bf), ((4, 2, HALF, W), bf), ((2, HALF, W), bf), ((2, 2, HALF, W), bf),
        ((T, W), fl), ((SL, CAP, WS), bf), ((SL, CAP, WS), bf),
        ((16, SL, CAP, W), bf), ((16, SL, CAP, W), bf), ((SL, F, W), bf), ((SL, F, W), bf), ((SL, F, W), bf),
        ((4 * CAP, F), fl), ((4 * CAP, F), fl), ((4 * CAP, F), bf),
        ((2, 4, 2, 2, CAP, W), bf), ((2, 4, 2, 2, 2, CAP, W), bf), ((2, 2, 2, CAP, W), bf), ((2, 2, 2, 2, CAP, W), bf),
        ((SL, CAP, W), bf), ((SL, CAP, W), bf),
    ]
    return pl.pallas_call(
        layer_kernel,
        out_shape=jax.ShapeDtypeStruct((T, W), bf),
        in_specs=[vmem] * 5 + [hbm, hbm] + [vmem] * 3 + [hbm] * 3,
        out_specs=vmem,
        scratch_shapes=[pltpu.VMEM(*s) for s in scratch]
        + [dma((SL + 1 + 3 * SL,)), dma((N_MAIL,)), dma((N_MAIL,)), dma((8,)), dma((8,)), dma((8,)), dma((8,))],
        compiler_params=pltpu.CompilerParams(collective_id=0, has_side_effects=True, vmem_limit_bytes=60 * 2**20),
        name="layer",
    )(queries, keys, values, log_decay.T, doc_ids.reshape(1, T), residual, out_weight, norm_gain.reshape(SL, W),
      expert_ids.T, route_weight.T, w_gate[0].T, w_up[0].T, w_down[0])


def solution(mesh):
    return jax.shard_map(
        shards,
        mesh=mesh,
        in_specs=(
            P("seq", "hx"),
            P("seq", "hx"),
            P("seq", "hx"),
            P("seq", "hx"),
            P("seq"),
            P("seq", None),
            P("hx", None),
            P(),
            P("seq", None),
            P("seq", None),
            P("hx", None, "seq"),
            P("hx", None, "seq"),
            P("hx", "seq", None),
        ),
        out_specs=P("seq", "hx"),
        check_vma=False,
    )
```

time: 327 us -> 154 us (0.47)
  waiting for transfers between devices: 98.2 us -> 0 us
  Pallas kernels: 97.2 us -> 151 us
  blocking collectives: 49.5 us -> 0 us
  local copies, waits for them, and re-layouts: 27.5 us -> 2.97 us
  starting transfers between devices: 15.8 us -> 0 us
  between operations: 15.5 us -> 0.01 us
  matrix products: 12 us -> 0 us
  other arithmetic: 9.13 us -> 0 us
    reduce_scatter x1 -> x0, waiting for transfers between devices: 90 us -> none  [shards(): lax.psum_scatter(jnp.dot(row_block, out_weight, preferred_element_type=jn...]
    pallas_call x1, Pallas kernels: 97.2 us -> 151 us  [shards(): pl.pallas_call(layer_kernel, out_shape=jax.ShapeDtypeStruct((T, W), bf),...]
    unnamed x1 -> x0, blocking collectives: 35.8 us -> none
    unnamed x17 -> x1, local copies, waits for them, and re-layouts: 18 us -> 1.62 us
    all_to_all x2 -> x0, starting transfers between devices: 15.8 us -> none  [the longest x1 8.68 us: shards(): lax.all_to_all(expert_out.astype(jnp.bfloat16), 'hx', split_axis=1, conca...]
    all_gather x1 -> x0, blocking collectives: 13.7 us -> none  [prefix(): lax.all_gather(a.astype(kind), axis)]
    dot_general x5 -> x0, matrix products: 12 us -> none  [the longest x1 7 us: shards(): jnp.dot(row_block, out_weight, preferred_element_type=jnp.float32)]
    all_to_all x2 -> x0, waiting for transfers between devices: 8.19 us -> none  [the longest x1 8.19 us: shards(): lax.all_to_all(expert_out.astype(jnp.bfloat16), 'hx', split_axis=1, conca...]
  transfers between devices with their start and end apart: 4 -> 0, of which waited for: 2 -> 0; matrix products, arithmetic and copies ran while one was open for 8% -> 0% of each run, Pallas kernels for 30% -> 0%
where the time goes in v2:
time: 154 us
  Pallas kernels  151 us (98%)
  local copies, waits for them, and re-layouts  2.97 us (2%)
    pallas_call x1, Pallas kernels, shards(): pl.pallas_call(layer_kernel, out_shape=jax.ShapeDtypeStruct((T, W), bf),...  151 us

profile of v2, /device:TPU:1, one launch (start us, length us, event | category | flops | bytes accessed | tf_op | source)
XLA Modules:
  0.0 153.7 jit_solution(3403415131264169487)
XLA Ops:
  0.0 1.3 reshape.7.gain
  1.4 150.7 %layer.1 = bf16[128,768]{1,0:T(8,128)(2,1)} custom-call(bf16[128,512]{1,0:T(8,128)(2,1)} %q.1, bf16[128,512]{1,0:T(8,128)(2,1)} %k.1, bf16[128,512]{1,0:T(8,128)(2,1)} %v.1, f32[4,128]{1,0:T(4,128)} %bitcast.14, s32[1,128]{1,0:T(1,128)} %bitcast.17, bf16[128,6144]{1,0:T(8,128)(2,1)} %residual_in.1, bf16[512,6144]{1,0:T(8,128)(2,1)} %wo_in.1, ...), custom_call_target="tpu_custom_call" | custom-call | tf_op jit(solution)/shard_map/layer/pallas_call | solution.py:526
  152.1 1.6 %copy.15 = bf16[128,768]{1,0:T(8,128)(2,1)} copy(bf16[128,768]{1,0:T(8,128)(2,1)} %layer.1) | data formatting | bytes 393216

commit v3 on v2

v3 whole, which is shorter than its diff:
```python
import jax
import jax.numpy as jnp
from jax import lax
from jax.experimental import pallas as pl
from jax.experimental.pallas import tpu as pltpu
from jax.sharding import PartitionSpec as P

MESH = pl.DeviceIdType.MESH
CAP = 40
HS = 128
HEADS = 4
T = 128
N_SEQ = 16
SL = 8
W = 768
HW = W // 2
F = 288
ORDER = [(0, 0), (1, 0), (3, 0), (0, 1), (0, 3), (1, 1), (1, 3), (3, 1), (3, 3), (2, 0), (0, 2), (1, 2), (3, 2), (2, 1), (2, 3), (2, 2)]
SLOT = {r: i for i, r in enumerate(ORDER)}


def at(half, first, second):
    return SLOT[(first % 4, second % 4) if half == 0 else (second % 4, first % 4)]


class Mail:
    def __init__(self, send_sem, recv_sem):
        self.send_sem, self.recv_sem = send_sem, recv_sem
        self.number, self.sent = {}, []

    def make(self, key, src, dst, device):
        n = self.number.setdefault(key, len(self.number))
        return pltpu.make_async_remote_copy(
            src_ref=src, dst_ref=dst, send_sem=self.send_sem.at[n], recv_sem=self.recv_sem.at[n],
            device_id=device, device_id_type=MESH)

    def send(self, key, src, dst, device):
        copy = self.make(key, src, dst, device)
        copy.start()
        self.sent.append(copy)

    def arrived(self, key, dst, device):
        self.make(key, dst, dst, device).wait_recv()

    def drain(self):
        for copy in self.sent:
            copy.wait_send()


def ring(half, seq):
    y, z = seq // 4, seq % 4
    yp, ym = ((y + 1) % 4) * 4 + z, ((y + 3) % 4) * 4 + z
    zp, zm = y * 4 + (z + 1) % 4, y * 4 + (z + 3) % 4
    ids = (yp, ym, zp, zm) if half == 0 else (zp, zm, yp, ym)
    return [{"seq": i} for i in ids]


def position(dx, turn):
    return 4 * (dx // 2) + dx % 2 + 2 * turn


class Gather:
    def __init__(self, mail, x, half, turn, seq):
        self.mail, self.x, self.half, self.turn = mail, x, half, turn
        self.fp, self.fm, self.sp, self.sm = ring(half, seq)

    def part(self, f, s, unit):
        lo = 4 * self.half + 2 * self.turn
        return self.x.at[at(self.half, f, s), pl.ds(lo, 2) if unit is None else pl.ds(lo + unit, 1)]

    def push(self, f, s, unit, device, tf, ts):
        key = ("g", self.half, self.turn, tf % 4, ts % 4, unit)
        self.mail.send(key, self.part(f, s, unit), self.part(tf, ts, unit), device)

    def got(self, f, s, unit):
        self.mail.arrived(("g", self.half, self.turn, f % 4, s % 4, unit), self.part(f, s, unit), self.fp)

    def across(self, f):
        self.push(f, 0, None, self.sp, f, 3)
        self.push(f, 0, None, self.sm, f, 1)

    def start(self):
        self.push(0, 0, None, self.fp, 3, 0)
        self.push(0, 0, None, self.fm, 1, 0)
        self.across(0)

    def first(self, f):
        self.got(f, 0, None)
        if f == 3:
            self.push(3, 0, 0, self.fp, 2, 0)
        else:
            self.push(1, 0, 1, self.fm, 2, 0)
        self.across(f)

    def first_far(self):
        self.got(2, 0, 0)
        self.got(2, 0, 1)
        self.across(2)

    def second(self, f):
        self.got(f, 3, None)
        self.push(f, 3, 0, self.sp, f, 2)
        self.got(f, 1, None)
        self.push(f, 1, 1, self.sm, f, 2)

    def second_far(self, f):
        self.got(f, 2, 0)
        self.got(f, 2, 1)


class Reduce:
    def __init__(self, mail, p, r1, r2, q1, q2, half, turn, seq):
        self.mail, self.p, self.half, self.turn = mail, p, half, turn
        self.r1, self.r2, self.q1, self.q2 = r1.at[half, turn], r2.at[half, turn], q1.at[half, turn], q2.at[half, turn]
        self.fp, self.fm, self.sp, self.sm = ring(half, seq)

    def unit(self, f, s, u):
        return self.p.at[at(self.half, f, s), 4 * self.half + 2 * self.turn + u]

    def push(self, key, src, dst, device):
        self.mail.send((self.half, self.turn) + key, src, dst, device)

    def got(self, key, dst):
        self.mail.arrived((self.half, self.turn) + key, dst, self.fp)
        return dst

    def total(self, f, s, u, *others):
        total = f32(self.unit(f, s, u)[...])
        for other in others:
            total += f32(other[...])
        return bf16(total)

    def add(self, f, s, u, *others):
        self.unit(f, s, u)[...] = self.total(f, s, u, *others)

    def start(self, f):
        self.push(("r1", f, 0), self.unit(f, 2, 0), self.r1.at[f, 0], self.sp)
        self.push(("r1", f, 1), self.unit(f, 2, 1), self.r1.at[f, 1], self.sm)
        self.push(("r2", f, 0, 1), self.unit(f, 1, 1), self.r2.at[f, 0, 1], self.sp)
        self.push(("r2", f, 1, 0), self.unit(f, 3, 0), self.r2.at[f, 1, 0], self.sm)

    def middle(self, f):
        self.add(f, 1, 0, self.got(("r1", f, 0), self.r1.at[f, 0]))
        self.push(("r2", f, 0, 0), self.unit(f, 1, 0), self.r2.at[f, 0, 0], self.sp)
        self.add(f, 3, 1, self.got(("r1", f, 1), self.r1.at[f, 1]))
        self.push(("r2", f, 1, 1), self.unit(f, 3, 1), self.r2.at[f, 1, 1], self.sm)

    def end(self, f):
        for u in (1, 0) if f == 1 else (0, 1):
            self.add(f, 0, u, self.got(("r2", f, 0, u), self.r2.at[f, 0, u]),
                     self.got(("r2", f, 1, u), self.r2.at[f, 1, u]))
            if f == 2:
                self.push(("q1", u), self.unit(2, 0, u), self.q1.at[u], (self.fp, self.fm)[u])
            if f == 1:
                if u == 0:
                    self.add(1, 0, 0, self.got(("q1", 0), self.q1.at[0]))
                self.push(("q2", 0, u), self.unit(1, 0, u), self.q2.at[0, u], self.fp)
            if f == 3:
                if u == 1:
                    self.add(3, 0, 1, self.got(("q1", 1), self.q1.at[1]))
                self.push(("q2", 1, u), self.unit(3, 0, u), self.q2.at[1, u], self.fm)

    def last(self, u, out):
        a = self.got(("q2", 0, u), self.q2.at[0, u])
        b = self.got(("q2", 1, u), self.q2.at[1, u])
        out[4 * self.half + 2 * self.turn + u] = self.total(0, 0, u, a, b)


def iota(shape, dim):
    return lax.broadcasted_iota(jnp.int32, shape, dim)


def lanes(n):
    return pl.ds(pl.multiple_of(n * W, W), W)


def f32(a):
    return a.astype(jnp.float32)


def bf16(a):
    return a.astype(jnp.bfloat16)


def dot(a, b, ca=1, cb=0, **kw):
    return lax.dot_general(a, b, (((ca,), (cb,)), ((), ())), preferred_element_type=jnp.float32, **kw)


def dispatch(ids):
    experts = iota((SL, T), 0)
    named = (ids[0:1, :] == experts) | (ids[1:2, :] == experts)
    before = bf16(jnp.where(iota((T, T), 0) < iota((T, T), 1), 1.0, 0.0))
    rank = dot(bf16(jnp.where(named, 1.0, 0.0)), before)
    slot = f32(iota((CAP, T), 0))
    chosen = f32(jnp.where(named, 1.0, 0.0))
    return [jnp.where(rank[e : e + 1, :] == slot, 1.0, 0.0) * chosen[e : e + 1, :] for e in range(SL)]


def greet(seq, x, c):
    others = [{"seq": (seq + d) % N_SEQ} for d in range(1, N_SEQ)]
    others += [{"hx": (2 * x + c + d) % SL} for d in range(1, SL)]
    barrier = pltpu.get_barrier_semaphore()
    for device in others:
        pl.semaphore_signal(barrier, inc=1, device_id=device, device_id_type=MESH)
    return lambda: pl.semaphore_wait(barrier, len(others))


def local_attention(q, k, v, decay, docs, states, head_out, carry):
    doc_row = jnp.broadcast_to(f32(docs[...]), (T, T))
    doc_col = doc_row.T
    allowed = (iota((T, T), 0) >= iota((T, T), 1)) & (doc_row == doc_col)
    upto = f32(jnp.where(iota((T, T), 0) <= iota((T, T), 1), 1.0, 0.0))
    rows = jnp.concatenate([decay[...], jnp.zeros((8 - HEADS, T), jnp.float32)], axis=0)
    sums = dot(rows, upto, precision=lax.Precision.HIGHEST)
    first, last = doc_col[0:1, :], doc_col[T - 1 : T, :]
    row = iota((16, HS), 0)
    for h in range(HEADS):
        lanes = slice(h * HS, (h + 1) * HS)
        across = jnp.broadcast_to(sums[h : h + 1, :], (T, T))
        down = across.T
        fade = jnp.where(allowed, jnp.exp(jnp.where(allowed, down - across, 0.0)), 0.0)
        scores = dot(q[:, lanes], k[:, lanes], 1, 1)
        head_out[h] = dot(bf16(scores * fade), v[:, lanes])
        total = down[T - 1 : T, :]
        to_end = jnp.where(doc_col == last, jnp.exp(total - down), 0.0)
        state = bf16(dot(bf16(f32(k[:, lanes]) * to_end), v[:, lanes], 0, 0))
        carry[h] = bf16(f32(q[:, lanes]) * jnp.where(doc_col == first, jnp.exp(down), 0.0))
        high = f32(bf16(total))
        mid = f32(bf16(total - high))
        low = total - high - mid
        facts = jnp.where(row == 0, high, jnp.where(row == 1, mid, jnp.where(row == 2, low, jnp.where(row == 3, first, last))))
        for part in range(4):
            states[4 * h + part, 0:32] = state[32 * part : 32 * (part + 1)]
            states[4 * h + part, 32:48] = bf16(facts)


def carry_states(mail, seq, states, arrived, entering, incoming):
    for d in range(1, N_SEQ):
        mail.send(("s", d), states.at[(seq + d) % N_SEQ], arrived.at[seq], {"seq": (seq + d) % N_SEQ})
    arrived[seq] = states[seq]
    for d in range(1, N_SEQ):
        mail.arrived(("s", d), arrived.at[(seq + N_SEQ - d) % N_SEQ], {"seq": (seq + d) % N_SEQ})
    state = jnp.zeros((32, HS), jnp.float32)
    before = jnp.full((1, HS), -1.0, jnp.float32)
    for s in range(N_SEQ):
        facts = f32(arrived[s, 32:48])
        log_total = facts[0:1] + facts[1:2] + facts[2:3]
        first, last = facts[3:4], facts[4:5]
        state = state * jnp.where(before == first, 1.0, 0.0)
        entering[s] = bf16(state)
        state = state * jnp.where(first == last, jnp.exp(log_total), 0.0) + f32(arrived[s, 0:32])
        before = last
    for d in range(1, N_SEQ):
        mail.send(("c", d), entering.at[(seq + d) % N_SEQ], incoming.at[seq], {"seq": (seq + d) % N_SEQ})
    incoming[seq] = entering[seq]
    for d in range(1, N_SEQ):
        mail.arrived(("c", d), incoming.at[(seq + N_SEQ - d) % N_SEQ], {"seq": (seq + d) % N_SEQ})


def attention_rows(head_out, carry, incoming, attn):
    for h in range(HEADS):
        state = incoming[4 * h : 4 * h + 4].reshape(HS, HS)
        out = head_out[h] + dot(carry[h], state)
        mean = jnp.mean(out * out, axis=1, keepdims=True)
        attn[:, h * HS : (h + 1) * HS] = bf16(out * lax.rsqrt(mean + 1e-05))


HALF = T // 2


class Project:
    def __init__(self, mail, x, c, turn, attn, wo, to_twin, from_twin, part, r1, r2, residual, hidden):
        self.mail, self.c, self.turn, self.attn, self.wo = mail, c, turn, attn, wo
        self.to_twin, self.from_twin, self.part = to_twin.at[turn], from_twin.at[turn], part.at[turn]
        self.r1, self.r2, self.residual, self.hidden = r1.at[turn], r2.at[turn], residual, hidden
        self.twin = {"hx": 2 * x + 1 - c}
        self.up, self.down = {"hx": 2 * ((x + 1) % 4) + c}, {"hx": 2 * ((x + 3) % 4) + c}
        self.lanes = slice(turn * HW, (turn + 1) * HW)

    def product(self, n):
        return dot(self.attn[...], self.wo[n, :, self.lanes]).reshape(2, HALF, HW)

    def send(self, key, src, dst, device):
        self.mail.send((self.turn,) + key, src, dst, device)

    def got(self, key, dst):
        self.mail.arrived((self.turn,) + key, dst, self.up)
        return f32(dst[...])

    def start(self):
        for dx in (2, 1, 3, 0):
            self.to_twin[dx] = bf16(self.product(2 * dx + 1 - self.c))
            self.send(("t", dx), self.to_twin.at[dx], self.from_twin.at[dx], self.twin)

    def both(self, dx):
        return self.product(2 * dx + self.c) + self.got(("t", dx), self.from_twin.at[dx])

    def away(self):
        part = self.part
        part[2] = bf16(self.both(2))
        self.send(("p1", 0), part.at[2, 0], self.r1.at[0], self.up)
        self.send(("p1", 1), part.at[2, 1], self.r1.at[1], self.down)
        mine = self.both(1)
        part[1, 1] = bf16(mine[1])
        self.send(("p2", 0, 1), part.at[1, 1], self.r2.at[0, 1], self.up)
        self.mine_up = mine[0]
        mine = self.both(3)
        part[3, 0] = bf16(mine[0])
        self.send(("p2", 1, 0), part.at[3, 0], self.r2.at[1, 0], self.down)
        self.mine_down = mine[1]
        self.mine = self.both(0)

    def onward(self):
        self.part[1, 0] = bf16(self.mine_up + self.got(("p1", 0), self.r1.at[0]))
        self.send(("p2", 0, 0), self.part.at[1, 0], self.r2.at[0, 0], self.up)
        self.part[3, 1] = bf16(self.mine_down + self.got(("p1", 1), self.r1.at[1]))
        self.send(("p2", 1, 1), self.part.at[3, 1], self.r2.at[1, 1], self.down)

    def home(self):
        for u in (1, 0):
            rows = slice(u * HALF, (u + 1) * HALF)
            total = f32(self.residual[rows, self.lanes]) + self.mine[u]
            total += self.got(("p2", 0, u), self.r2.at[0, u])
            total += self.got(("p2", 1, u), self.r2.at[1, u])
            self.hidden[rows, self.lanes] = total


class Cross:
    def __init__(self, send_sem, recv_sem, number, x, c):
        self.send_sem, self.recv_sem, self.base, self.x, self.c, self.sent = send_sem, recv_sem, 8 * number, x, c, []

    def make(self, dx, to, own, src, dst):
        return pltpu.make_async_remote_copy(
            src_ref=src, dst_ref=dst, send_sem=self.send_sem.at[self.base + 2 * dx + to],
            recv_sem=self.recv_sem.at[self.base + 2 * dx + own], device_id={"hx": 2 * ((self.x + dx) % 4) + to}, device_id_type=MESH)

    def send(self, dx, to, src, dst):
        copy = self.make(dx, to, self.c, src, dst)
        copy.start()
        self.sent.append(copy)

    def arrived(self, dx, own, dst):
        self.make(dx, own, own, dst, dst).wait_recv()

    def drain(self):
        for copy in self.sent:
            copy.wait_send()


def rows_to_experts(cross, facts, x, c, turn, hidden, gain, pick, out, facts_out, block, facts_in):
    hx = 2 * x + c
    own = pl.ds(pl.multiple_of(hx * W + turn * HW, 128), HW)
    rows = bf16(hidden[:, turn * HW : (turn + 1) * HW] * gain[:, own])
    if turn == 1:
        square = jnp.sum(hidden[...] * hidden[...], axis=1, keepdims=True)
        high = f32(bf16(square))
        rows = jnp.concatenate([rows, bf16(jnp.where(iota((T, 128), 1) < 64, high, square - high))], axis=1)
    for dx, to in ((2, 0), (2, 1), (1, 0), (1, 1), (3, 0), (3, 1), (0, 1 - c)):
        n = 2 * dx + (to if dx else 0)
        slots = bf16(dot(pick[2 * ((x + dx) % 4) + to], rows))
        if turn == 1:
            facts_out[n] = slots[:, HW:]
            facts.send(dx, to, facts_out.at[n], facts_in.at[2 * ((4 - dx) % 4) + c])
        out[turn, n] = slots[:, :HW]
        cross.send(dx, to, out.at[turn, n], block.at[position((4 - dx) % 4, turn), c])
    slots = bf16(dot(pick[hx], rows))
    block[position(0, turn), c] = slots[:, :HW]
    if turn == 1:
        facts_in[c] = slots[:, HW:]


def from_row(cross, c, place):
    cross.arrived(0, 1 - c, place(0, 1 - c))
    for dx in (1, 3, 2):
        for own in (0, 1):
            cross.arrived(dx, own, place(4 - dx, own))


def send_scale(mail, seq, facts_in, scale_out, scales):
    square = sum(f32(facts_in[k]) for k in range(SL))
    mean = (square[:, 0:1] + square[:, 64:65]) * (1.0 / (SL * W))
    scale = lax.rsqrt(mean + 1e-06)
    row = jnp.sum(jnp.where(iota((CAP, 128), 0) == iota((CAP, 128), 1), scale, 0.0), axis=0, keepdims=True)
    scale_out[...] = jnp.broadcast_to(row, (8, 128))
    scales[0] = jnp.broadcast_to(row, (8, 128))
    for dy, dz in ORDER[1:]:
        device = {"seq": ((seq // 4 + dy) % 4) * 4 + (seq % 4 + dz) % 4}
        place = SLOT[((4 - dy) % 4, (4 - dz) % 4)]
        mail.send(("n", place), scale_out, scales.at[place], device)


def scale_column(scales, group):
    own = iota((CAP, 128), 0) == iota((CAP, 128), 1)
    return jnp.concatenate(
        [jnp.sum(jnp.where(own, scales[4 * group + b, 0:1, :], 0.0), axis=1, keepdims=True) for b in range(4)], axis=0)


def run_experts(mail, seq, rows, p, wgu, wd, acc, act, scales, r1, r2, q1, q2, loads, out, first_rows, second_rows, finish, combine):
    gathers = [[Gather(mail, rows, half, turn, seq) for half in (0, 1)] for turn in (0, 1)]
    reduces = [[Reduce(mail, p, r1, r2, q1, q2, half, turn, seq) for half in (0, 1)] for turn in (0, 1)]

    def up(group, turn):
        blocks = slice(4 * group, 4 * group + 4)
        parts = [rows[blocks, position(n // 2, turn), n % 2].reshape(4 * CAP, HW) for n in range(SL)]
        block = jnp.concatenate(parts, axis=1)
        total = dot(block, wgu[turn], 1, 1)
        if turn == 0:
            acc[group] = total
        else:
            total = (total + acc[group]) * scale_column(scales, group)
            gate = total[:, 0:F]
            act[group] = bf16(gate / (1.0 + jnp.exp(-gate)) * total[:, F : 2 * F])

    def down(group, turn):
        blocks = slice(4 * group, 4 * group + 4)
        for dx in range(4):
            block = dot(act[group], wd[turn, :, dx * W : (dx + 1) * W])
            for core in (0, 1):
                half = block[:, core * HW : (core + 1) * HW]
                p[blocks, position(dx, turn), core] = bf16(half.reshape(4, CAP, HW))

    def each(step, turn, *args, of=gathers):
        for one in of[turn]:
            getattr(one, step)(*args)

    def reduce(turn, *steps):
        for step in steps:
            each({"s": "start", "m": "middle", "e": "end"}[step[0]], turn, int(step[1]), of=reduces)

    def end(turn):
        for u in (1, 0):
            for half in (1, 0):
                reduces[turn][half].last(u, out)
                finish(2 * half + u, turn)

    first_rows()
    each("start", 0)
    second_rows()
    each("first", 0, 3)
    each("first", 0, 1)
    each("second", 0, 0)
    each("first_far", 0)
    second_rows(True)
    each("start", 1)
    each("second", 0, 3)
    each("second", 0, 1)
    for copy in loads:
        copy.wait()
    up(0, 0)
    each("first", 1, 3)
    each("first", 1, 1)
    each("second", 0, 2)
    each("second", 1, 0)
    up(1, 0)
    for f in (0, 3, 1):
        each("second_far", 0, f)
    each("first_far", 1)
    up(2, 0)
    each("second", 1, 3)
    each("second", 1, 1)
    each("second_far", 0, 2)
    up(3, 0)
    for place in range(1, N_SEQ):
        mail.arrived(("n", place), scales.at[place], {"seq": (seq + 1) % N_SEQ})
    up(0, 1)
    down(0, 0)
    each("second", 1, 2)
    up(1, 1)
    down(1, 0)
    for f in (0, 3, 1):
        each("second_far", 1, f)
    up(2, 1)
    down(2, 0)
    each("second_far", 1, 2)
    up(3, 1)
    down(3, 0)

    reduce(0, "s2", "s1")
    down(0, 1)
    reduce(0, "m2", "s3")
    down(1, 1)
    reduce(0, "m1", "e2", "s0")
    down(2, 1)
    down(3, 1)
    reduce(0, "m3")
    reduce(1, "s2")
    reduce(0, "e1", "m0")
    reduce(1, "s1")
    reduce(0, "e3")
    reduce(1, "m2")
    reduce(0, "e0")
    reduce(1, "s3", "m1")
    end(0)
    reduce(1, "e2", "s0", "m3", "e1", "m0", "e3", "e0")
    combine(0)
    end(1)
    combine(1)


def layer_kernel(q, k, v, decay, docs, residual_in, wo_in, gain, ids, weights, wg_in, wu_in, wd_in, result,
                 wo, residual, pick, states, arrived, entering, incoming, head_out, carry, attn,
                 to_twin, from_twin, part, s1, s2, hidden, slot_out, facts_out, facts_in, scale_out, scales,
                 rows, p, wgu, wd, acc, act, r1, r2, q1, q2, done, back,
                 load_sem, send_sem, recv_sem, cross_send, cross_recv):
    seq, hx = lax.axis_index("seq"), lax.axis_index("hx")
    x, c = hx // 2, hx % 2

    arrive = greet(seq, x, c)
    front, loads = [], []

    def load(copies, source, target):
        n = len(front) + len(loads)
        copies.append(pltpu.make_async_copy(source, target, load_sem.at[n]))
        copies[-1].start()

    for n in range(SL):
        load(front, wo_in.at[:, lanes(2 * ((x + n // 2) % 4) + n % 2)], wo.at[n])
    load(front, residual_in.at[:, lanes(hx)], residual)
    for turn in (0, 1):
        for n in range(SL):
            slice_at = (2 * ((x + n // 2) % 4) + n % 2) * W + turn * HW
            here, target = pl.ds(pl.multiple_of(slice_at, 128), HW), slice(n * HW, (n + 1) * HW)
            load(loads, wg_in.at[:, here], wgu.at[turn, 0:F, target])
            load(loads, wu_in.at[:, here], wgu.at[turn, F : 2 * F, target])
            load(loads, wd_in.at[:, here], wd.at[turn, :, target])

    mail = Mail(send_sem, recv_sem)
    local_attention(q, k, v, decay, docs, states, head_out, carry)
    fill_pick(ids, pick)
    arrive()
    carry_states(mail, seq, states, arrived, entering, incoming)
    attention_rows(head_out, carry, incoming, attn)
    for copy in front:
        copy.wait()
    projects = [Project(mail, x, c, turn, attn, wo, to_twin, from_twin, part, s1, s2, residual, hidden) for turn in (0, 1)]
    crosses = [Cross(cross_send, cross_recv, number, x, c) for number in range(5)]
    own = rows.at[0]

    def dispatch(turn):
        rows_to_experts(crosses[turn], crosses[2], x, c, turn, hidden, gain, pick, slot_out, facts_out, own, facts_in)

    def first_rows():
        projects[0].start()
        projects[0].away()
        projects[1].start()
        projects[0].onward()
        projects[1].away()
        projects[0].home()
        dispatch(0)
        projects[1].onward()
        from_row(crosses[0], c, lambda dx, core: own.at[position(dx, 0), core])

    def second_rows(here=False):
        if here:
            from_row(crosses[2], c, lambda dx, core: facts_in.at[2 * dx + core])
            send_scale(mail, seq, facts_in, scale_out, scales)
            from_row(crosses[1], c, lambda dx, core: own.at[position(dx, 1), core])
        else:
            projects[1].home()
            dispatch(1)

    def finish(dx, turn):
        for to in (0, 1) if dx else (1 - c,):
            crosses[3 + turn].send(dx, to, done.at[position(dx, turn), to], back.at[turn, hx])
        if dx == 0:
            back[turn, hx] = done[position(0, turn), c]

    def combine(turn):
        weighted = []
        for e in range(SL):
            share = jnp.where(ids[0:1, :] == e, weights[0:1, :], 0.0) + jnp.where(ids[1:2, :] == e, weights[1:2, :], 0.0)
            weighted.append(f32(pick[e]) * share)
        weighted = jnp.concatenate(weighted, axis=0)
        high = bf16(weighted)
        low = bf16(weighted - f32(high))
        from_row(crosses[3 + turn], c, lambda dx, core: back.at[turn, 2 * ((x + dx) % 4) + core])
        expert_out = bf16(f32(back[turn]).reshape(SL * CAP, HW))
        half = slice(turn * HW, (turn + 1) * HW)
        result[:, half] = bf16(hidden[:, half] + dot(high, expert_out, 0, 0) + dot(low, expert_out, 0, 0))

    run_experts(mail, seq, rows, p, wgu, wd, acc, act, scales, r1, r2, q1, q2, loads, done,
                first_rows, second_rows, finish, combine)
    mail.drain()
    for cross in crosses:
        cross.drain()


def fill_pick(ids, pick):
    for e, block in enumerate(dispatch(ids)):
        pick[e] = bf16(block)


N_MAIL = 30 + 15 + 2 * (4 + 6 + 40 + 48 + 12)


def shards(queries, keys, values, log_decay, doc_ids, residual, out_weight, norm_gain, expert_ids, route_weight, w_gate, w_up, w_down):
    vmem = pl.BlockSpec(memory_space=pltpu.VMEM)
    hbm = pl.BlockSpec(memory_space=pl.ANY)
    bf, fl = jnp.bfloat16, jnp.float32
    dma = pltpu.SemaphoreType.DMA
    unit = (2, CAP, HW)
    scratch = [
        ((SL, HEADS * HS, W), bf), ((T, W), bf), ((SL, CAP, T), bf),
        ((N_SEQ, 48, HS), bf), ((N_SEQ, 48, HS), bf), ((N_SEQ, 32, HS), bf), ((N_SEQ, 32, HS), bf),
        ((HEADS, T, HS), fl), ((HEADS, T, HS), bf), ((T, HEADS * HS), bf),
        ((2, 4, 2, HALF, HW), bf), ((2, 4, 2, HALF, HW), bf), ((2, 4, 2, HALF, HW), bf),
        ((2, 2, HALF, HW), bf), ((2, 2, 2, HALF, HW), bf),
        ((T, W), fl), ((2, SL, CAP, HW), bf), ((SL, CAP, 128), bf), ((SL, CAP, 128), bf), ((8, 128), fl), ((16, 8, 128), fl),
        ((16, SL) + unit, bf), ((16, SL) + unit, bf), ((2, 2 * F, 4 * W), bf), ((2, F, 4 * W), bf),
        ((4, 4 * CAP, 2 * F), fl), ((4, 4 * CAP, F), bf),
        ((2, 2, 4, 2) + unit, bf), ((2, 2, 4, 2, 2) + unit, bf), ((2, 2, 2) + unit, bf), ((2, 2, 2, 2) + unit, bf),
        ((SL,) + unit, bf), ((2, SL, CAP, HW), bf),
    ]
    return pl.pallas_call(
        layer_kernel,
        out_shape=jax.ShapeDtypeStruct((T, W), bf),
        in_specs=[vmem] * 5 + [hbm, hbm] + [vmem] * 3 + [hbm] * 3,
        out_specs=vmem,
        scratch_shapes=[pltpu.VMEM(*s) for s in scratch]
        + [dma((SL + 1 + 6 * SL,)), dma((N_MAIL,)), dma((N_MAIL,)), dma((40,)), dma((40,))],
        compiler_params=pltpu.CompilerParams(collective_id=0, has_side_effects=True, vmem_limit_bytes=60 * 2**20),
        name="layer",
    )(queries, keys, values, log_decay.T, doc_ids.reshape(1, T), residual, out_weight, norm_gain.reshape(1, SL * W),
      expert_ids.T, route_weight.T, w_gate[0].T, w_up[0].T, w_down[0])


def solution(mesh):
    return jax.shard_map(
        shards,
        mesh=mesh,
        in_specs=(
            P("seq", "hx"),
            P("seq", "hx"),
            P("seq", "hx"),
            P("seq", "hx"),
            P("seq"),
            P("seq", None),
            P("hx", None),
            P(),
            P("seq", None),
            P("seq", None),
            P("hx", None, "seq"),
            P("hx", None, "seq"),
            P("hx", "seq", None),
        ),
        out_specs=P("seq", "hx"),
        check_vma=False,
    )
```

time: 154 us -> 140 us (0.909)
  Pallas kernels: 151 us -> 139 us
    pallas_call x1, Pallas kernels: 151 us -> 139 us  [shards(): pl.pallas_call(layer_kernel, out_shape=jax.ShapeDtypeStruct((T, W), bf),...]
where the time goes in v3:
time: 140 us
  Pallas kernels  139 us (99%)
  local copies, waits for them, and re-layouts  1.62 us (1%)
    pallas_call x1, Pallas kernels, shards(): pl.pallas_call(layer_kernel, out_shape=jax.ShapeDtypeStruct((T, W), bf),...  139 us

profile of v3, /device:TPU:1, one launch (start us, length us, event | category | flops | bytes accessed | tf_op | source)
XLA Modules:
  0.0 140.2 jit_solution(7617709012016256054)
XLA Ops:
  0.0 138.6 %layer.1 = bf16[128,768]{1,0:T(8,128)(2,1)} custom-call(bf16[128,512]{1,0:T(8,128)(2,1)} %q.1, bf16[128,512]{1,0:T(8,128)(2,1)} %k.1, bf16[128,512]{1,0:T(8,128)(2,1)} %v.1, f32[4,128]{1,0:T(4,128)} %bitcast.16, s32[1,128]{1,0:T(1,128)} %bitcast.19, bf16[128,6144]{1,0:T(8,128)(2,1)} %residual_in.1, bf16[512,6144]{1,0:T(8,128)(2,1)} %wo_in.1, ...), custom_call_target="tpu_custom_call" | custom-call | tf_op jit(solution)/shard_map/layer/pallas_call | solution.py:614
  138.6 1.6 %copy.15 = bf16[128,768]{1,0:T(8,128)(2,1)} copy(bf16[128,768]{1,0:T(8,128)(2,1)} %layer.1) | data formatting | bytes 393216

commit v4 on v3

--- a/solution.py
+++ b/solution.py
@@ -15,12 +15,19 @@
 W = 768
 HW = W // 2
 F = 288
-ORDER = [(0, 0), (1, 0), (3, 0), (0, 1), (0, 3), (1, 1), (1, 3), (3, 1), (3, 3), (2, 0), (0, 2), (1, 2), (3, 2), (2, 1), (2, 3), (2, 2)]
+ORDER = [(0, 0), (1, 0), (3, 0), (0, 1), (0, 3), (1, 1), (1, 3), (3, 1), (3, 3), (2, 0), (0, 2), (3, 2), (1, 2), (2, 3), (2, 1), (2, 2)]
 SLOT = {r: i for i, r in enumerate(ORDER)}
 
 
 def at(half, first, second):
     return SLOT[(first % 4, second % 4) if half == 0 else (second % 4, first % 4)]
+
+
+def across_plane(seq, dy, dz):
+    return (seq // 4 + dy) % 4 * 4 + (seq % 4 + dz) % 4
+
+
+FAR_FIRST = sorted(ORDER[1:], key=lambda r: -(min(r[0], 4 - r[0]) + min(r[1], 4 - r[1])))
 
 
 class Mail:
@@ -197,7 +204,7 @@
 
 
 def greet(seq, x, c):
-    others = [{"seq": (seq + d) % N_SEQ} for d in range(1, N_SEQ)]
+    others = [{"seq": across_plane(seq, *r)} for r in FAR_FIRST]
     others += [{"hx": (2 * x + c + d) % SL} for d in range(1, SL)]
     barrier = pltpu.get_barrier_semaphore()
     for device in others:
@@ -235,11 +242,12 @@
 
 
 def carry_states(mail, seq, states, arrived, entering, incoming):
-    for d in range(1, N_SEQ):
-        mail.send(("s", d), states.at[(seq + d) % N_SEQ], arrived.at[seq], {"seq": (seq + d) % N_SEQ})
+    for r in FAR_FIRST:
+        to = across_plane(seq, *r)
+        mail.send(("s", r), states.at[to], arrived.at[seq], {"seq": to})
     arrived[seq] = states[seq]
-    for d in range(1, N_SEQ):
-        mail.arrived(("s", d), arrived.at[(seq + N_SEQ - d) % N_SEQ], {"seq": (seq + d) % N_SEQ})
+    for r in reversed(FAR_FIRST):
+        mail.arrived(("s", r), arrived.at[across_plane(seq, 4 - r[0], 4 - r[1])], {"seq": across_plane(seq, *r)})
     state = jnp.zeros((32, HS), jnp.float32)
     before = jnp.full((1, HS), -1.0, jnp.float32)
     for s in range(N_SEQ):
@@ -250,11 +258,12 @@
         entering[s] = bf16(state)
         state = state * jnp.where(first == last, jnp.exp(log_total), 0.0) + f32(arrived[s, 0:32])
         before = last
-    for d in range(1, N_SEQ):
-        mail.send(("c", d), entering.at[(seq + d) % N_SEQ], incoming.at[seq], {"seq": (seq + d) % N_SEQ})
+    for r in FAR_FIRST:
+        to = across_plane(seq, *r)
+        mail.send(("c", r), entering.at[to], incoming.at[seq], {"seq": to})
     incoming[seq] = entering[seq]
-    for d in range(1, N_SEQ):
-        mail.arrived(("c", d), incoming.at[(seq + N_SEQ - d) % N_SEQ], {"seq": (seq + d) % N_SEQ})
+    for r in reversed(FAR_FIRST):
+        mail.arrived(("c", r), incoming.at[across_plane(seq, 4 - r[0], 4 - r[1])], {"seq": across_plane(seq, *r)})
 
 
 def attention_rows(head_out, carry, incoming, attn):
@@ -467,10 +476,11 @@
     each("second", 1, 2)
     up(1, 1)
     down(1, 0)
-    for f in (0, 3, 1):
-        each("second_far", 1, f)
+    each("second_far", 1, 0)
+    each("second_far", 1, 3)
     up(2, 1)
     down(2, 0)
+    each("second_far", 1, 1)
     each("second_far", 1, 2)
     up(3, 1)
     down(3, 0)
@@ -498,7 +508,7 @@
 
 
 def layer_kernel(q, k, v, decay, docs, residual_in, wo_in, gain, ids, weights, wg_in, wu_in, wd_in, result,
-                 wo, residual, pick, states, arrived, entering, incoming, head_out, carry, attn,
+                 wo, residual, pick, shares, states, arrived, entering, incoming, head_out, carry, attn,
                  to_twin, from_twin, part, s1, s2, hidden, slot_out, facts_out, facts_in, scale_out, scales,
                  rows, p, wgu, wd, acc, act, r1, r2, q1, q2, done, back,
                  load_sem, send_sem, recv_sem, cross_send, cross_recv):
@@ -526,7 +536,7 @@
 
     mail = Mail(send_sem, recv_sem)
     local_attention(q, k, v, decay, docs, states, head_out, carry)
-    fill_pick(ids, pick)
+    fill_pick(ids, weights, pick, shares)
     arrive()
     carry_states(mail, seq, states, arrived, entering, incoming)
     attention_rows(head_out, carry, incoming, attn)
@@ -566,17 +576,11 @@
             back[turn, hx] = done[position(0, turn), c]
 
     def combine(turn):
-        weighted = []
-        for e in range(SL):
-            share = jnp.where(ids[0:1, :] == e, weights[0:1, :], 0.0) + jnp.where(ids[1:2, :] == e, weights[1:2, :], 0.0)
-            weighted.append(f32(pick[e]) * share)
-        weighted = jnp.concatenate(weighted, axis=0)
-        high = bf16(weighted)
-        low = bf16(weighted - f32(high))
+        both = shares[...].reshape(2, SL * CAP, T)
         from_row(crosses[3 + turn], c, lambda dx, core: back.at[turn, 2 * ((x + dx) % 4) + core])
         expert_out = bf16(f32(back[turn]).reshape(SL * CAP, HW))
         half = slice(turn * HW, (turn + 1) * HW)
-        result[:, half] = bf16(hidden[:, half] + dot(high, expert_out, 0, 0) + dot(low, expert_out, 0, 0))
+        result[:, half] = bf16(hidden[:, half] + sum(dot(both[part], expert_out, 0, 0) for part in (0, 1)))
 
     run_experts(mail, seq, rows, p, wgu, wd, acc, act, scales, r1, r2, q1, q2, loads, done,
                 first_rows, second_rows, finish, combine)
@@ -585,9 +589,13 @@
         cross.drain()
 
 
-def fill_pick(ids, pick):
+def fill_pick(ids, weights, pick, shares):
     for e, block in enumerate(dispatch(ids)):
         pick[e] = bf16(block)
+        share = jnp.where(ids[0:1, :] == e, weights[0:1, :], 0.0) + jnp.where(ids[1:2, :] == e, weights[1:2, :], 0.0)
+        high = bf16(block * share)
+        shares[0, e] = high
+        shares[1, e] = bf16(block * share - f32(high))
 
 
 N_MAIL = 30 + 15 + 2 * (4 + 6 + 40 + 48 + 12)
@@ -600,7 +608,7 @@
     dma = pltpu.SemaphoreType.DMA
     unit = (2, CAP, HW)
     scratch = [
-        ((SL, HEADS * HS, W), bf), ((T, W), bf), ((SL, CAP, T), bf),
+        ((SL, HEADS * HS, W), bf), ((T, W), bf), ((SL, CAP, T), bf), ((2, SL, CAP, T), bf),
         ((N_SEQ, 48, HS), bf), ((N_SEQ, 48, HS), bf), ((N_SEQ, 32, HS), bf), ((N_SEQ, 32, HS), bf),
         ((HEADS, T, HS), fl), ((HEADS, T, HS), bf), ((T, HEADS * HS), bf),
         ((2, 4, 2, HALF, HW), bf), ((2, 4, 2, HALF, HW), bf), ((2, 4, 2, HALF, HW), bf),

time: 140 us -> 139 us (level)
  no operation moved by 1% of the time
where the time goes in v4:
time: 139 us
  Pallas kernels  138 us (99%)
  local copies, waits for them, and re-layouts  1.62 us (1%)
    pallas_call x1, Pallas kernels, shards(): pl.pallas_call(layer_kernel, out_shape=jax.ShapeDtypeStruct((T, W), bf),...  138 us

profile of v4, /device:TPU:1, one launch (start us, length us, event | category | flops | bytes accessed | tf_op | source)
XLA Modules:
  0.0 139.3 jit_solution(10264329320463111950)
XLA Ops:
  0.0 137.7 %layer.1 = bf16[128,768]{1,0:T(8,128)(2,1)} custom-call(bf16[128,512]{1,0:T(8,128)(2,1)} %q.1, bf16[128,512]{1,0:T(8,128)(2,1)} %k.1, bf16[128,512]{1,0:T(8,128)(2,1)} %v.1, f32[4,128]{1,0:T(4,128)} %bitcast.16, s32[1,128]{1,0:T(1,128)} %bitcast.19, bf16[128,6144]{1,0:T(8,128)(2,1)} %residual_in.1, bf16[512,6144]{1,0:T(8,128)(2,1)} %wo_in.1, ...), custom_call_target="tpu_custom_call" | custom-call | tf_op jit(solution)/shard_map/layer/pallas_call | solution.py:622
  137.7 1.6 %copy.15 = bf16[128,768]{1,0:T(8,128)(2,1)} copy(bf16[128,768]{1,0:T(8,128)(2,1)} %layer.1) | data formatting | bytes 393216

commit v5 on v4

--- a/solution.py
+++ b/solution.py
@@ -420,9 +420,9 @@
             gate = total[:, 0:F]
             act[group] = bf16(gate / (1.0 + jnp.exp(-gate)) * total[:, F : 2 * F])
 
-    def down(group, turn):
+    def down(group, turn, chips=(0, 1, 2, 3)):
         blocks = slice(4 * group, 4 * group + 4)
-        for dx in range(4):
+        for dx in chips:
             block = dot(act[group], wd[turn, :, dx * W : (dx + 1) * W])
             for core in (0, 1):
                 half = block[:, core * HW : (core + 1) * HW]
@@ -483,9 +483,10 @@
     each("second_far", 1, 1)
     each("second_far", 1, 2)
     up(3, 1)
-    down(3, 0)
-
-    reduce(0, "s2", "s1")
+    for half in (0, 1):
+        down(3, 0, (2 * half, 2 * half + 1))
+        reduces[0][half].start(2)
+    reduce(0, "s1")
     down(0, 1)
     reduce(0, "m2", "s3")
     down(1, 1)

time: 139 us -> 140 us (level)
  no operation moved by 1% of the time
where the time goes in v5:
time: 140 us; the launch traced here: 139 us
  Pallas kernels  138 us (99%)
  local copies, waits for them, and re-layouts  1.62 us (1%)
    pallas_call x1, Pallas kernels, shards(): pl.pallas_call(layer_kernel, out_shape=jax.ShapeDtypeStruct((T, W), bf),...  138 us

profile of v5, /device:TPU:1, one launch (start us, length us, event | category | flops | bytes accessed | tf_op | source)
XLA Modules:
  0.0 139.5 jit_solution(9426857225173449083)
XLA Ops:
  0.0 137.9 %layer.1 = bf16[128,768]{1,0:T(8,128)(2,1)} custom-call(bf16[128,512]{1,0:T(8,128)(2,1)} %q.1, bf16[128,512]{1,0:T(8,128)(2,1)} %k.1, bf16[128,512]{1,0:T(8,128)(2,1)} %v.1, f32[4,128]{1,0:T(4,128)} %bitcast.16, s32[1,128]{1,0:T(1,128)} %bitcast.19, bf16[128,6144]{1,0:T(8,128)(2,1)} %residual_in.1, bf16[512,6144]{1,0:T(8,128)(2,1)} %wo_in.1, ...), custom_call_target="tpu_custom_call" | custom-call | tf_op jit(solution)/shard_map/layer/pallas_call | solution.py:623
  137.9 1.6 %copy.15 = bf16[128,768]{1,0:T(8,128)(2,1)} copy(bf16[128,768]{1,0:T(8,128)(2,1)} %layer.1) | data formatting | bytes 393216

commit v6 on v4

--- a/solution.py
+++ b/solution.py
@@ -507,8 +507,8 @@
     combine(1)
 
 
-def layer_kernel(q, k, v, decay, docs, residual_in, wo_in, gain, ids, weights, wg_in, wu_in, wd_in, result,
-                 wo, residual, pick, shares, states, arrived, entering, incoming, head_out, carry, attn,
+def layer_kernel(q_in, k_in, v_in, decay_in, docs_in, residual_in, wo_in, gain_in, ids_in, weights_in, wg_in, wu_in, wd_in, result,
+                 q, k, v, decay, docs, gain, ids, weights, wo, residual, pick, shares, states, arrived, entering, incoming, head_out, carry, attn,
                  to_twin, from_twin, part, s1, s2, hidden, slot_out, facts_out, facts_in, scale_out, scales,
                  rows, p, wgu, wd, acc, act, r1, r2, q1, q2, done, back,
                  load_sem, send_sem, recv_sem, cross_send, cross_recv):
@@ -516,13 +516,16 @@
     x, c = hx // 2, hx % 2
 
     arrive = greet(seq, x, c)
-    front, loads = [], []
+    early, front, loads = [], [], []
 
     def load(copies, source, target):
-        n = len(front) + len(loads)
+        n = len(early) + len(front) + len(loads)
         copies.append(pltpu.make_async_copy(source, target, load_sem.at[n]))
         copies[-1].start()
 
+    sources = (q_in, k_in, v_in, decay_in, docs_in, gain_in, ids_in, weights_in)
+    for source, target in zip(sources, (q, k, v, decay, docs, gain, ids, weights)):
+        load(early, source, target)
     for n in range(SL):
         load(front, wo_in.at[:, lanes(2 * ((x + n // 2) % 4) + n % 2)], wo.at[n])
     load(front, residual_in.at[:, lanes(hx)], residual)
@@ -535,6 +538,8 @@
             load(loads, wd_in.at[:, here], wd.at[turn, :, target])
 
     mail = Mail(send_sem, recv_sem)
+    for copy in early:
+        copy.wait()
     local_attention(q, k, v, decay, docs, states, head_out, carry)
     fill_pick(ids, weights, pick, shares)
     arrive()
@@ -608,6 +613,8 @@
     dma = pltpu.SemaphoreType.DMA
     unit = (2, CAP, HW)
     scratch = [
+        ((T, HEADS * HS), bf), ((T, HEADS * HS), bf), ((T, HEADS * HS), bf), ((HEADS, T), fl), ((1, T), jnp.int32),
+        ((1, SL * W), fl), ((2, T), jnp.int32), ((2, T), fl),
         ((SL, HEADS * HS, W), bf), ((T, W), bf), ((SL, CAP, T), bf), ((2, SL, CAP, T), bf),
         ((N_SEQ, 48, HS), bf), ((N_SEQ, 48, HS), bf), ((N_SEQ, 32, HS), bf), ((N_SEQ, 32, HS), bf),
         ((HEADS, T, HS), fl), ((HEADS, T, HS), bf), ((T, HEADS * HS), bf),
@@ -622,10 +629,10 @@
     return pl.pallas_call(
         layer_kernel,
         out_shape=jax.ShapeDtypeStruct((T, W), bf),
-        in_specs=[vmem] * 5 + [hbm, hbm] + [vmem] * 3 + [hbm] * 3,
+        in_specs=[hbm] * 13,
         out_specs=vmem,
         scratch_shapes=[pltpu.VMEM(*s) for s in scratch]
-        + [dma((SL + 1 + 6 * SL,)), dma((N_MAIL,)), dma((N_MAIL,)), dma((40,)), dma((40,))],
+        + [dma((SL + SL + 1 + 6 * SL,)), dma((N_MAIL,)), dma((N_MAIL,)), dma((40,)), dma((40,))],
         compiler_params=pltpu.CompilerParams(collective_id=0, has_side_effects=True, vmem_limit_bytes=60 * 2**20),
         name="layer",
     )(queries, keys, values, log_decay.T, doc_ids.reshape(1, T), residual, out_weight, norm_gain.reshape(1, SL * W),

time: 139 us -> 138 us (level)
  no operation moved by 1% of the time
where the time goes in v6:
time: 138 us
  Pallas kernels  137 us (99%)
  local copies, waits for them, and re-layouts  1.62 us (1%)
    pallas_call x1, Pallas kernels, shards(): pl.pallas_call(layer_kernel, out_shape=jax.ShapeDtypeStruct((T, W), bf),...  137 us

profile of v6, /device:TPU:1, one launch (start us, length us, event | category | flops | bytes accessed | tf_op | source)
XLA Modules:
  0.0 138.3 jit_solution(9099736069611786674)
XLA Ops:
  0.0 136.7 %layer.1 = bf16[128,768]{1,0:T(8,128)(2,1)} custom-call(bf16[128,512]{1,0:T(8,128)(2,1)} %q_in.1, bf16[128,512]{1,0:T(8,128)(2,1)} %k_in.1, bf16[128,512]{1,0:T(8,128)(2,1)} %v_in.1, f32[4,128]{1,0:T(4,128)} %bitcast.16, s32[1,128]{1,0:T(1,128)} %bitcast.19, bf16[128,6144]{1,0:T(8,128)(2,1)} %residual_in.1, bf16[512,6144]{1,0:T(8,128)(2,1)} %wo_in.1, ...), custom_call_target="tpu_custom_call" | custom-call | tf_op jit(solution)/shard_map/layer/pallas_call | solution.py:629
  136.7 1.6 %copy.15 = bf16[128,768]{1,0:T(8,128)(2,1)} copy(bf16[128,768]{1,0:T(8,128)(2,1)} %layer.1) | data formatting | bytes 393216
